TPU v7x, 32 devices: a whole 2x2x4 slice. The times are simulated.
32 devices in a mesh: dp: 4 (over z), hidden: 8 (over y, x, core).
Axes of the slice: x: 2, y: 2, z: 4, core: 2. Of those that a mesh axis runs over, the one named last changes fastest.
Arguments:
- tokens: bfloat16 [128, 4096], P('dp', 'hidden'), may hold values from -6 to 6
- grad_out: bfloat16 [128, 4096], P('dp', 'hidden'), may hold values from -6 to 6
- routes: int32 [128, 2], P('dp'), may hold values from 0 to 3, all different within a row; in each aligned block of 32 rows (0 to 31, 32 to 63, ...) at most 20 rows name the same one
- probs: bfloat16 [128, 2], P('dp'), may hold values from 0.099609375 to 0.8984375
- gate_weight: bfloat16 [28672, 4096], P(('dp', 'hidden')), may hold values from -0.09375 to 0.09375
- up_weight: bfloat16 [28672, 4096], P(('dp', 'hidden')), may hold values from -0.09375 to 0.09375
- down_weight: bfloat16 [28672, 4096], P(('dp', 'hidden')), may hold values from -0.0625 to 0.0625
Outputs:
- grad_tokens: bfloat16 [128, 4096], P('dp', 'hidden')
- grad_probs: float32 [128, 2], P('dp')
- grad_gate: bfloat16 [28672, 4096], P(('dp', 'hidden'))
- grad_up: bfloat16 [28672, 4096], P(('dp', 'hidden'))
Inputs may be any that keep to these rules, and one draw needn't show every extreme that they name: `routes`: A token's two experts differ. Among the 32 tokens of one index of dp no expert is named more than 20 times, a bound that some block reaches.
All inputs are finite; a program needn't handle non-finite values.
Results may differ from a plain program's by a relative error of at most 0.0049.
Values may be sent and summed in bfloat16 or wider, within the bound.
A program may use at most 128 MiB of HBM per device.

v0:
```python
import jax
import jax.numpy as jnp
from jax import lax
from jax.sharding import PartitionSpec as P

CAP = 20


def body(tokens, grad_out, routes, probs, gate_weight, up_weight, down_weight):
    dp_count = lax.axis_size("dp")
    hidden_count = lax.axis_size("hidden")
    large_count = dp_count // 6
    expert_total = dp_count - 3 * large_count
    block_ids = jnp.arange(dp_count, dtype=jnp.int32)
    owners = jnp.where(block_ids < 4 * large_count, block_ids // 4, block_ids - 3 * large_count)
    expert_hits = (
        routes[:, :, None] == jnp.arange(expert_total, dtype=jnp.int32)[None, None, :]
    ).astype(jnp.int32)
    per_token = jnp.sum(expert_hits, axis=1)
    before = jnp.cumsum(per_token, axis=0) - per_token
    slot_rank = jnp.sum(expert_hits * before[:, None, :], axis=2)
    matches = routes[:, :, None] == owners[None, None, :]
    slot_hits = slot_rank[:, :, None, None] == jnp.arange(CAP, dtype=jnp.int32)[None, None, None, :]
    picked = (matches[:, :, :, None] & slot_hits).astype(jnp.float32)
    select = jnp.sum(picked, axis=1)
    select_half = select.astype(jnp.bfloat16)
    send_tokens = jnp.einsum(
        "tjc,td->jcd", select_half, tokens, preferred_element_type=jnp.float32
    ).astype(jnp.bfloat16)
    send_grads = jnp.einsum(
        "tjc,td->jcd", select_half, grad_out, preferred_element_type=jnp.float32
    ).astype(jnp.bfloat16)
    send_probs = jnp.einsum(
        "tkjc,tk->jc", picked, probs.astype(jnp.float32), precision=lax.Precision.HIGHEST
    ).astype(jnp.bfloat16)
    recv_tokens, recv_grads, recv_probs = (
        lax.all_to_all(send_tokens, "dp", split_axis=0, concat_axis=0, tiled=True),
        lax.all_to_all(send_grads, "dp", split_axis=0, concat_axis=0, tiled=True),
        lax.all_to_all(send_probs, "dp", split_axis=0, concat_axis=0, tiled=True),
    )
    row_count = dp_count * CAP
    contract = (((1,), (1,)), ((), ()))
    full_tokens, full_grads = (
        lax.all_gather(recv_tokens, "hidden", axis=2, tiled=True),
        lax.all_gather(recv_grads, "hidden", axis=2, tiled=True),
    )
    token_rows = full_tokens.reshape(row_count, full_tokens.shape[2])
    grad_rows = full_grads.reshape(row_count, full_grads.shape[2])
    back_pre = lax.dot_general(grad_rows, down_weight, contract, preferred_element_type=jnp.float32)
    slot_probs = recv_probs.reshape(row_count).astype(jnp.float32)
    gate_pre = lax.dot_general(
        token_rows, gate_weight, contract, preferred_element_type=jnp.float32
    )
    up_pre = lax.dot_general(token_rows, up_weight, contract, preferred_element_type=jnp.float32)
    sigmoid_gate = jax.nn.sigmoid(gate_pre)
    silu_gate = gate_pre * sigmoid_gate
    router_part = jnp.sum(silu_gate * up_pre * back_pre, axis=1)
    scaled = slot_probs[:, None] * back_pre
    grad_gate_pre = (
        scaled * up_pre * sigmoid_gate * (1.0 + gate_pre * (1.0 - sigmoid_gate))
    ).astype(jnp.bfloat16)
    grad_up_pre = (scaled * silu_gate).astype(jnp.bfloat16)
    over_rows = (((0,), (0,)), ((), ()))
    grad_gate = lax.dot_general(
        grad_gate_pre, token_rows, over_rows, preferred_element_type=jnp.float32
    ).astype(jnp.bfloat16)
    grad_up = lax.dot_general(
        grad_up_pre, token_rows, over_rows, preferred_element_type=jnp.float32
    ).astype(jnp.bfloat16)
    feature_width = gate_weight.shape[1] // hidden_count
    cross = (((0,), (1,)), ((), ()))
    own_features = lax.psum_scatter(
        lax.dot_general(gate_weight, grad_gate_pre, cross, preferred_element_type=jnp.float32)
        + lax.dot_general(up_weight, grad_up_pre, cross, preferred_element_type=jnp.float32),
        "hidden",
        scatter_dimension=0,
        tiled=True,
    ).T
    router_payload = lax.psum(router_part, "hidden")
    back_features, back_router = (
        lax.all_to_all(
            own_features.reshape(dp_count, CAP, feature_width),
            "dp",
            split_axis=0,
            concat_axis=0,
            tiled=True,
        ),
        lax.all_to_all(
            router_payload.reshape(dp_count, CAP), "dp", split_axis=0, concat_axis=0, tiled=True
        ),
    )
    token_router = jnp.einsum("tkjc,jc->tk", picked, back_router, precision=lax.Precision.HIGHEST)
    grad_tokens = jnp.einsum(
        "tjc,jcd->td", select, back_features, precision=lax.Precision.HIGHEST
    ).astype(jnp.bfloat16)
    return (grad_tokens, token_router, grad_gate, grad_up)


def solution(mesh):
    placed = (
        P("dp", "hidden"),
        P("dp", "hidden"),
        P("dp", None),
        P("dp", None),
        P(("dp", "hidden"), None),
        P(("dp", "hidden"), None),
        P(("dp", "hidden"), None),
    )
    return jax.shard_map(
        body,
        mesh=mesh,
        in_specs=placed,
        out_specs=(
            P("dp", "hidden"),
            P("dp", None),
            P(("dp", "hidden"), None),
            P(("dp", "hidden"), None),
        ),
        check_vma=False,
    )
```

profile of v0, /device:TPU:0, one launch (start us, length us, event | category | flops | bytes accessed | tf_op | source)
XLA Modules:
  0.0 139.8 jit_solution(1307754142305787071)
XLA Ops:
  7.2 0.0 copy-start
  7.2 0.0 slice-start.2
  7.2 0.8 iota_compare_fusion.1
  8.0 0.8 convert_reduce_fusion.1
  8.8 0.1 copy.16
  8.9 0.1 reduce_window_sum.11
  9.0 0.1 copy.18
  9.1 0.7 select_reduce_fusion
  9.8 0.8 fusion.3
  10.6 0.6 copy.19
  11.2 6.3 %all-to-all-start = ((bf16[4,1,20]{2,1,0:T(2,128)(2,1)}), bf16[4,1,20]{2,1,0:T(2,128)(2,1)S(1)}, u32[]{:S(2)}, u32[]{:S(2)}) async-start(bf16[4,1,20]{2,1,0:T(2,128)(2,1)} %copy.19), calls=%async_computation | async-start | bytes 4096 | tf_op jit(solution)/shard_map/all_to_all | solution.py:39
  17.6 0.0 copy-done
  17.6 0.8 convolution_convert_fusion.3
  18.4 4.6 %all-to-all-done = bf16[4,1,20]{2,1,0:T(2,128)(2,1)S(1)} async-done(((bf16[4,1,20]{2,1,0:T(2,128)(2,1)}), bf16[4,1,20]{2,1,0:T(2,128)(2,1)S(1)}, u32[]{:S(2)}, u32[]{:S(2)}) %all-to-all-start) | async-done | bytes 192 | tf_op jit(solution)/shard_map/all_to_all | solution.py:39
  23.0 3.3 %all-to-all-start.1 = ((bf16[4,20,512]{2,1,0:T(8,128)(2,1)}), bf16[4,20,512]{2,1,0:T(8,128)(2,1)S(1)}, u32[]{:S(2)}, u32[]{:S(2)}) async-start(bf16[4,20,512]{2,1,0:T(8,128)(2,1)} %convolution_convert_fusion.3), calls=%async_computation.1 | async-start | bytes 196608 | tf_op jit(solution)/shard_map/all_to_all | solution.py:38
  26.3 1.6 %convolution_convert_fusion.2 = bf16[4,20,512]{2,1,0:T(8,128)(2,1)} fusion(bf16[32,512]{1,0:T(8,128)(2,1)} %param.7, bf16[32,4,20]{0,1,2:T(4,128)(2,1)S(1)} %convert_element_type.49), kind=kOutput, calls=%fused_computation.4 | convolution fusion | flops 2662400 | bytes 119808 | tf_op jit(solution)/shard_map/tjc,td->jcd/dot_general | solution.py:27
  27.9 0.1 reshape.56
  28.0 4.1 %all-to-all-done.1 = bf16[4,20,512]{2,1,0:T(8,128)(2,1)S(1)} async-done(((bf16[4,20,512]{2,1,0:T(8,128)(2,1)}), bf16[4,20,512]{2,1,0:T(8,128)(2,1)S(1)}, u32[]{:S(2)}, u32[]{:S(2)}) %all-to-all-start.1) | async-done | bytes 81952 | tf_op jit(solution)/shard_map/all_to_all | solution.py:38
  32.1 3.3 %all-to-all-start.2 = ((bf16[4,20,512]{2,1,0:T(8,128)(2,1)}), bf16[4,20,512]{2,1,0:T(8,128)(2,1)S(1)}, u32[]{:S(2)}, u32[]{:S(2)}) async-start(bf16[4,20,512]{2,1,0:T(8,128)(2,1)} %convolution_convert_fusion.2), calls=%async_computation.2 | async-start | bytes 196608 | tf_op jit(solution)/shard_map/all_to_all | solution.py:37
  35.5 0.0 reduce-scatter.2.cloned.1.call-start
  35.5 11.5 %all_gather.6 = bf16[4,20,4096]{2,1,0:T(8,128)(2,1)} all-gather(bf16[4,20,512]{2,1,0:T(8,128)(2,1)S(1)} %all-to-all-done.1), channel_id=1, replica_groups=mesh['dp'=4,'hidden'=8] {'hidden'}, dimensions={2}, use_global_device_ids=true | all-gather | bytes 737280 | tf_op jit(solution)/shard_map/all_gather | solution.py:45
  47.0 2.1 %reshape.53 = bf16[80,4096]{1,0:T(8,128)(2,1)} reshape(bf16[4,20,4096]{2,1,0:T(8,128)(2,1)} %all_gather.6) | data formatting | bytes 1310720 | tf_op jit(solution)/shard_map/reshape | solution.py:48
  49.1 0.0 all-to-all-done.2
  49.1 11.3 %all_gather.7 = bf16[4,20,4096]{2,1,0:T(8,128)(2,1)} all-gather(bf16[4,20,512]{2,1,0:T(8,128)(2,1)S(1)} %all-to-all-done.2), channel_id=1, replica_groups=mesh['dp'=4,'hidden'=8] {'hidden'}, dimensions={2}, use_global_device_ids=true | all-gather | bytes 737280 | tf_op jit(solution)/shard_map/all_gather | solution.py:44
  60.4 2.1 %reshape.54 = bf16[80,4096]{1,0:T(8,128)(2,1)} reshape(bf16[4,20,4096]{2,1,0:T(8,128)(2,1)} %all_gather.7) | data formatting | bytes 1310720 | tf_op jit(solution)/shard_map/reshape | solution.py:47
  62.6 0.0 slice-start.3
  62.6 0.0 copy-start.1
  62.6 0.0 copy-start.3
  62.6 5.8 %fusion.14 = f32[80,896]{1,0:T(8,128)S(1)} fusion(bf16[80,4096]{1,0:T(8,128)(2,1)} %reshape.54, bf16[896,4096]{1,0:T(8,128)(2,1)} %param.11), kind=kOutput, calls=%fused_computation.33 | convolution fusion | flops 587202560 | bytes 8282112 | tf_op jit(solution)/shard_map/dot_general | solution.py:51
  68.3 0.0 slice-done.2
  68.3 0.0 slice-done.3
  68.4 0.0 copy-done.1
  68.4 0.0 slice-start
  68.4 2.3 %fusion.13 = f32[80,896]{1,0:T(8,128)S(1)} fusion(bf16[80,4096]{1,0:T(8,128)(2,1)S(1)} %copy-done.1, bf16[896,4096]{1,0:T(8,128)(2,1)S(1)} %bitcast.48), kind=kOutput, calls=%fused_computation.32 | convolution fusion | flops 587202560 | bytes 8282112 | tf_op jit(solution)/shard_map/dot_general | solution.py:54
  70.7 0.0 copy-done.3
  70.7 0.0 slice-start.1
  70.7 5.7 %multiply_reduce_fusion = (f32[80]{0:T(128)S(1)}, bf16[80,896]{1,0:T(8,128)(2,1)S(1)}, bf16[80,896]{1,0:T(8,128)(2,1)S(1)}) fusion(f32[80,896]{1,0:T(8,128)S(1)} %fusion.13, f32[80,896]{1,0:T(8,128)S(1)} %fusion.14, f32[80]{0:T(128)S(1)} %reshape.56, bf16[80,4096]{1,0:T(8,128)(2,1)S(1)} %copy-done.3, bf16[896,4096]{1,0:T(8,128)(2,1)} %param.13), kind=kOutput, calls=%fused_computation.8 | convolution fusion | flops 588421056 | bytes 8856192 | tf_op jit(solution)/shard_map/dot_general | solution.py:49
  76.5 0.0 slice-done
  76.5 0.0 slice-done.1
  76.5 1.5 %fusion.15 = f32[80,4096]{1,0:T(8,128)S(1)} fusion(bf16[80,896]{1,0:T(8,128)(2,1)S(1)} %get-tuple-element.5, bf16[896,4096]{1,0:T(8,128)(2,1)S(1)} %bitcast.46), kind=kOutput, calls=%fused_computation.34 | convolution fusion | flops 587202560 | bytes 8794112 | tf_op jit(solution)/shard_map/dot_general | solution.py:73
  78.0 2.5 %fusion = f32[4096,80]{0,1:T(8,128)} fusion(f32[80,4096]{1,0:T(8,128)S(1)} %fusion.15, bf16[80,896]{1,0:T(8,128)(2,1)S(1)} %get-tuple-element.6, bf16[896,4096]{1,0:T(8,128)(2,1)S(1)} %bitcast.48), kind=kOutput, calls=%fused_computation.3 | convolution fusion | flops 587530240 | bytes 10104832 | tf_op jit(solution)/shard_map/dot_general | solution.py:74
  80.5 0.0 copy-start.2
  80.5 0.0 reduce-scatter.2.cloned.1.call-update
  80.5 0.1 all_to_all.28
  80.6 13.9 %psum.7 = f32[4,1,20]{2,0,1:T(4,128)} all-reduce(f32[4,1,20]{2,0,1:T(4,128)S(1)} %all_to_all.28), channel_id=1, replica_groups=mesh['dp'=4,'hidden'=8] {'hidden'}, use_global_device_ids=true, to_apply=%region_6.7 | all-reduce | flops 80 | bytes 640 | tf_op jit(solution)/shard_map/psum | solution.py:79
  94.6 5.0 %all-to-all-start.4 = ((f32[4,1,20]{2,1,0:T(1,128)}), f32[4,1,20]{2,1,0:T(1,128)S(1)}, u32[]{:S(2)}, u32[]{:S(2)}) async-start(f32[4,1,20]{2,1,0:T(1,128)} %bitcast.9), calls=%async_computation.5 | async-start | bytes 4096 | tf_op jit(solution)/shard_map/all_to_all | solution.py:88
  99.6 6.2 %convolution_convert_fusion = bf16[896,4096]{1,0:T(8,128)(2,1)} fusion(bf16[80,896]{1,0:T(8,128)(2,1)S(1)} %get-tuple-element.6, bf16[80,4096]{1,0:T(8,128)(2,1)} %reshape.54), kind=kOutput, calls=%fused_computation | convolution fusion | flops 590872576 | bytes 8138752 | tf_op jit(solution)/shard_map/dot_general | solution.py:67
  105.8 12.7 %reduce-scatter.2.cloned.1.call-done = f32[512,80]{0,1:T(8,128)} async-done(((f32[4096,80]{0,1:T(8,128)}), f32[512,80]{0,1:T(8,128)}) %reduce-scatter.2.cloned.1.call-update) | async-done | bytes 163856 | tf_op jit(solution)/shard_map/reduce_scatter | solution.py:72
  118.5 1.6 %reshape.55 = f32[4,20,512]{2,1,0:T(8,128)} reshape(f32[80,512]{1,0:T(8,128)} %bitcast.49) | data formatting | bytes 327680 | tf_op jit(solution)/shard_map/reshape | solution.py:82
  120.1 0.0 all-to-all-done.4
  120.1 4.6 %all-to-all-start.3 = ((f32[4,20,512]{2,1,0:T(8,128)}), f32[4,20,512]{2,1,0:T(8,128)S(1)}, u32[]{:S(2)}, u32[]{:S(2)}) async-start(f32[4,20,512]{2,1,0:T(8,128)} %reshape.55), calls=%async_computation.4 | async-start | bytes 393216 | tf_op jit(solution)/shard_map/all_to_all | solution.py:81
  124.7 0.0 copy-done.2
  124.7 5.1 %convolution_convert_fusion.1 = bf16[896,4096]{1,0:T(8,128)(2,1)} fusion(bf16[80,896]{1,0:T(8,128)(2,1)S(1)} %get-tuple-element.5, bf16[80,4096]{1,0:T(8,128)(2,1)S(1)} %copy-done.2), kind=kOutput, calls=%fused_computation.1 | convolution fusion | flops 590872576 | bytes 8138752 | tf_op jit(solution)/shard_map/dot_general | solution.py:64
  129.9 0.8 fusion.5
  130.6 1.5 %all-to-all-done.3 = f32[4,20,512]{2,1,0:T(8,128)S(1)} async-done(((f32[4,20,512]{2,1,0:T(8,128)}), f32[4,20,512]{2,1,0:T(8,128)S(1)}, u32[]{:S(2)}, u32[]{:S(2)}) %all-to-all-start.3) | async-done | bytes 163872 | tf_op jit(solution)/shard_map/all_to_all | solution.py:81
  132.1 0.9 fusion.1
  (9 shorter events, 0.1 us)
Async XLA Ops:
  7.2 10.5 %copy-start = (bf16[32,512]{1,0:T(8,128)(2,1)S(1)}, bf16[32,512]{1,0:T(8,128)(2,1)}, u32[]{:S(2)}) copy-start(bf16[32,512]{1,0:T(8,128)(2,1)} %param.8) | copy-start | bytes 98308
  7.2 61.2 %slice-start.2 = ((s8[7340032]{0:T(1024)(128)(4,1)}), s8[3145728]{0:T(1024)(128)(4,1)S(1)}, s32[]{:S(2)}) async-start(s8[7340032]{0:T(1024)(128)(4,1)} %bitcast.47), calls=%async_computation.9 | async-start | bytes 6291456
  11.2 11.8 %all-to-all-start = ((bf16[4,1,20]{2,1,0:T(2,128)(2,1)}), bf16[4,1,20]{2,1,0:T(2,128)(2,1)S(1)}, u32[]{:S(2)}, u32[]{:S(2)}) async-start(bf16[4,1,20]{2,1,0:T(2,128)(2,1)} %copy.19), calls=%async_computation | async-start | bytes 4096 | tf_op jit(solution)/shard_map/all_to_all | solution.py:39
  23.0 9.1 %all-to-all-start.1 = ((bf16[4,20,512]{2,1,0:T(8,128)(2,1)}), bf16[4,20,512]{2,1,0:T(8,128)(2,1)S(1)}, u32[]{:S(2)}, u32[]{:S(2)}) async-start(bf16[4,20,512]{2,1,0:T(8,128)(2,1)} %convolution_convert_fusion.3), calls=%async_computation.1 | async-start | bytes 196608 | tf_op jit(solution)/shard_map/all_to_all | solution.py:38
  32.1 17.0 %all-to-all-start.2 = ((bf16[4,20,512]{2,1,0:T(8,128)(2,1)}), bf16[4,20,512]{2,1,0:T(8,128)(2,1)S(1)}, u32[]{:S(2)}, u32[]{:S(2)}) async-start(bf16[4,20,512]{2,1,0:T(8,128)(2,1)} %convolution_convert_fusion.2), calls=%async_computation.2 | async-start | bytes 196608 | tf_op jit(solution)/shard_map/all_to_all | solution.py:37
  35.5 83.1 %reduce-scatter.2.cloned.1.call-start = ((), (), s32[]{:S(2)}) async-start(), calls=%async_computation.6 | async-start | bytes 1474560 | tf_op jit(solution)/shard_map/reduce_scatter | solution.py:72
  62.6 5.8 %slice-start.3 = ((s8[7340032]{0:T(1024)(128)(4,1)}), s8[4194304]{0:T(1024)(128)(4,1)S(1)}, s32[]{:S(2)}) async-start(s8[7340032]{0:T(1024)(128)(4,1)} %bitcast.47), calls=%async_computation.10 | async-start | bytes 8388608
  62.6 5.8 %copy-start.1 = (bf16[80,4096]{1,0:T(8,128)(2,1)S(1)}, bf16[80,4096]{1,0:T(8,128)(2,1)}, u32[]{:S(2)}) copy-start(bf16[80,4096]{1,0:T(8,128)(2,1)} %reshape.54) | copy-start | bytes 1966084
  62.6 8.2 %copy-start.3 = (bf16[80,4096]{1,0:T(8,128)(2,1)S(1)}, bf16[80,4096]{1,0:T(8,128)(2,1)}, u32[]{:S(2)}) copy-start(bf16[80,4096]{1,0:T(8,128)(2,1)} %reshape.53) | copy-start | bytes 1966084
  68.4 8.1 %slice-start = ((s8[7340032]{0:T(1024)(128)(4,1)}), s8[4194304]{0:T(1024)(128)(4,1)S(1)}, s32[]{:S(2)}) async-start(s8[7340032]{0:T(1024)(128)(4,1)} %bitcast.45), calls=%async_computation.7 | async-start | bytes 8388608
  70.7 5.8 %slice-start.1 = ((s8[7340032]{0:T(1024)(128)(4,1)}), s8[3145728]{0:T(1024)(128)(4,1)S(1)}, s32[]{:S(2)}) async-start(s8[7340032]{0:T(1024)(128)(4,1)} %bitcast.45), calls=%async_computation.8 | async-start | bytes 6291456
  80.5 44.2 %copy-start.2 = (bf16[80,4096]{1,0:T(8,128)(2,1)S(1)}, bf16[80,4096]{1,0:T(8,128)(2,1)}, u32[]{:S(2)}) copy-start(bf16[80,4096]{1,0:T(8,128)(2,1)} %reshape.54) | copy-start | bytes 1966084
  94.6 25.5 %all-to-all-start.4 = ((f32[4,1,20]{2,1,0:T(1,128)}), f32[4,1,20]{2,1,0:T(1,128)S(1)}, u32[]{:S(2)}, u32[]{:S(2)}) async-start(f32[4,1,20]{2,1,0:T(1,128)} %bitcast.9), calls=%async_computation.5 | async-start | bytes 4096 | tf_op jit(solution)/shard_map/all_to_all | solution.py:88
  120.1 12.0 %all-to-all-start.3 = ((f32[4,20,512]{2,1,0:T(8,128)}), f32[4,20,512]{2,1,0:T(8,128)S(1)}, u32[]{:S(2)}, u32[]{:S(2)}) async-start(f32[4,20,512]{2,1,0:T(8,128)} %reshape.55), calls=%async_computation.4 | async-start | bytes 393216 | tf_op jit(solution)/shard_map/all_to_all | solution.py:81
Sparse Core Ops, SparseCore 0:
  80.7 37.7 reduce-scatter.1
where the time goes:
time: 141 us; the launch traced here: 140 us
  blocking collectives  36.8 us (26%)
  matrix products  34 us (24%)
  waiting for transfers between devices  22.9 us (16%)
  starting transfers between devices  22.6 us (16%)
  between operations  14.2 us (10%)
  local copies, waits for them, and re-layouts  6.82 us (5%)
  other arithmetic  2.53 us (2%)
    psum x1, blocking collectives, body(): router_payload = lax.psum(router_part, 'hidden')  13.9 us
    reduce_scatter x1, waiting for transfers between devices, body(): lax.psum_scatter(lax.dot_general(gate_weight, grad_gate_pre, cross, prefe...  12.7 us
    all_gather x1, blocking collectives, body(): lax.all_gather(recv_grads, 'hidden', axis=2, tiled=True)  11.5 us
    all_gather x1, blocking collectives, body(): lax.all_gather(recv_tokens, 'hidden', axis=2, tiled=True)  11.3 us
    all_to_all x1, starting transfers between devices, body(): lax.all_to_all(send_probs, 'dp', split_axis=0, concat_axis=0, tiled=True)  6.32 us
    dot_general x1, matrix products, body(): lax.dot_general(grad_up_pre, token_rows, over_rows, preferred_element_typ...  6.23 us
    dot_general x1, matrix products, body(): lax.dot_general(token_rows, gate_weight, contract, preferred_element_type...  5.77 us
    dot_general x1, matrix products, body(): lax.dot_general(grad_rows, down_weight, contract, preferred_element_type=...  5.73 us
  transfers between devices with their start and end apart: 6, of which 4 were waited for; matrix products, arithmetic and copies ran while one was open for 13% of the time, Pallas kernels for 0%

commit v1 on v0

--- a/solution.py
+++ b/solution.py
@@ -1,6 +1,10 @@
+import functools
+
 import jax
 import jax.numpy as jnp
 from jax import lax
+from jax.experimental import pallas as pl
+from jax.experimental.pallas import tpu as pltpu
 from jax.sharding import PartitionSpec as P
 
 CAP = 20
@@ -96,6 +100,530 @@
     return (grad_tokens, token_router, grad_gate, grad_up)
 
 
+LANES = 128
+MESH = pl.DeviceIdType.MESH
+F32 = jnp.float32
+BF16 = jnp.bfloat16
+NT = (((1,), (1,)), ((), ()))
+NN = (((1,), (0,)), ((), ()))
+TN = (((0,), (0,)), ((), ()))
+
+
+def fits(dp_count, hidden_count, token_shape, weight_shape):
+    rows, width = token_shape
+    groups = width // LANES
+    return (
+        hidden_count == 8
+        and 2 <= dp_count <= 8
+        and width % LANES == 0
+        and rows * groups == LANES
+        and (CAP * groups) % 16 == 0
+        and (CAP * dp_count) % 16 == 0
+        and CAP * dp_count <= LANES
+        and weight_shape[0] % LANES == 0
+    )
+
+
+def dot(a, b, dims):
+    return lax.dot_general(a, b, dims, preferred_element_type=F32)
+
+
+def steps_of(values, size, count):
+    total = jnp.zeros_like(values)
+    for edge in range(1, count):
+        total = total + (values >= edge * size).astype(jnp.int32)
+    return total
+
+
+def fused_kernel(
+    dp_count,
+    owners,
+    routes_ref,
+    probs_ref,
+    tokens_ref,
+    grads_ref,
+    gate_hbm,
+    up_hbm,
+    down_hbm,
+    grad_tokens_ref,
+    grad_probs_ref,
+    x_out,
+    d_out,
+    weights,
+    weight_sem,
+    xbuf,
+    x_send,
+    x_recv,
+    zsend,
+    zrecv,
+    z_send_sem,
+    z_recv_sem,
+    aux_send,
+    aux_recv,
+    aux_send_sem,
+    aux_recv_sem,
+    acc,
+    dbuf,
+    one_send,
+    one_recv,
+    one_send_sem,
+    one_recv_sem,
+    two_send,
+    two_recv,
+    two_send_sem,
+    two_recv_sem,
+    own_part,
+    q_send,
+    q_recv,
+    q_send_sem,
+    q_recv_sem,
+    back_send,
+    back_recv,
+    back_send_sem,
+    back_recv_sem,
+    qz_send,
+    qz_recv,
+    qz_send_sem,
+    qz_recv_sem,
+    out_sem,
+):
+    rows, width = tokens_ref.shape
+    groups = width // LANES
+    packed = CAP * groups
+    slots = CAP * dp_count
+    plane = lax.axis_index("dp")
+    h = lax.axis_index("hidden")
+    core = h % 2
+    x_pos = (h // 2) % 2
+    y_pos = h // 4
+    to_sib = 1 - 2 * core
+    sib = h + to_sib
+    hx = h + 2 - 4 * x_pos
+    hy = h + 4 - 8 * y_pos
+    hd = hx + 4 - 8 * y_pos
+
+    def at_hidden(index):
+        return (plane, index)
+
+    def at_plane(step):
+        other = (plane + step) % dp_count
+        return other, (other, h)
+
+    barrier = pltpu.get_barrier_semaphore()
+    for index in (sib, hx, hy, hd):
+        pl.semaphore_signal(barrier, inc=1, device_id=at_hidden(index), device_id_type=MESH)
+    for step in range(1, dp_count):
+        pl.semaphore_signal(barrier, inc=1, device_id=at_plane(step)[1], device_id_type=MESH)
+
+    order = (h, sib, hx, hy, hx + to_sib, hy + to_sib, hd, hd + to_sib)
+
+    def weight_copy(which, index):
+        columns = pl.ds(pl.multiple_of(index * width, width), width)
+        source = (gate_hbm, up_hbm, down_hbm)[which]
+        return pltpu.make_async_copy(
+            source.at[:, columns], weights.at[which, index], weight_sem.at[which, index]
+        )
+
+    for index in order:
+        for which in range(3):
+            weight_copy(which, index).start()
+
+    pending = []
+
+    def send(source, target, send_sem, recv_sem, device):
+        copy = pltpu.make_async_remote_copy(
+            src_ref=source,
+            dst_ref=target,
+            send_sem=send_sem,
+            recv_sem=recv_sem,
+            device_id=device,
+            device_id_type=MESH,
+        )
+        copy.start()
+        pending.append(copy)
+
+    def arrived(target, send_sem, recv_sem):
+        pltpu.make_async_remote_copy(
+            src_ref=target,
+            dst_ref=target,
+            send_sem=send_sem,
+            recv_sem=recv_sem,
+            device_id=at_hidden(sib),
+            device_id_type=MESH,
+        ).wait_recv()
+
+    block_row = lax.broadcasted_iota(jnp.int32, (8, rows), 0)
+    owner_of = jnp.full((8, rows), -1, jnp.int32)
+    for j, owner in enumerate(owners):
+        owner_of = jnp.where(block_row == j, owner, owner_of)
+    first = jnp.broadcast_to(routes_ref[0:1, :], (8, rows))
+    second = jnp.broadcast_to(routes_ref[1:2, :], (8, rows))
+    prob_rows = probs_ref[...].astype(F32)
+    match = (owner_of == first) | (owner_of == second)
+    earlier = lax.broadcasted_iota(jnp.int32, (rows, rows), 0) < lax.broadcasted_iota(
+        jnp.int32, (rows, rows), 1
+    )
+    rank = dot(match.astype(F32).astype(BF16), earlier.astype(F32).astype(BF16), NN)
+    rank = jnp.where(match, rank, -1.0)
+    block_prob = jnp.where(owner_of == first, jnp.broadcast_to(prob_rows[0:1, :], (8, rows)), 0.0)
+    block_prob = block_prob + jnp.where(
+        owner_of == second, jnp.broadcast_to(prob_rows[1:2, :], (8, rows)), 0.0
+    )
+    for j in range(dp_count):
+        aux_send[j] = jnp.zeros((8, LANES), F32)
+        aux_send[j, 0:1, 0:rows] = rank[j : j + 1, :]
+        aux_send[j, 1:2, 0:rows] = block_prob[j : j + 1, :]
+    wide_rank = jnp.concatenate([rank] * groups, axis=1)
+    pack_row = lax.broadcasted_iota(jnp.int32, (packed, LANES), 0)
+    pack_group = steps_of(pack_row, CAP, groups)
+    pack_slot = (pack_row - CAP * pack_group).astype(F32)
+    lane_group = steps_of(lax.broadcasted_iota(jnp.int32, (packed, LANES), 1), rows, groups)
+    same_group = pack_group == lane_group
+    select = jnp.concatenate(
+        [
+            jnp.where(
+                same_group & (pack_slot == jnp.broadcast_to(wide_rank[j : j + 1, :], pack_slot.shape)),
+                1.0,
+                0.0,
+            )
+            for j in range(dp_count)
+        ],
+        axis=0,
+    ).astype(BF16)
+
+    for a, ref in enumerate((tokens_ref, grads_ref)):
+        stacked = jnp.concatenate(
+            [ref[:, n * LANES : (n + 1) * LANES] for n in range(groups)], axis=0
+        )
+        zsend[a] = dot(select, stacked, NN).astype(BF16).reshape(dp_count, packed, LANES)
+        zrecv[a, plane] = zsend[a, plane]
+        if a == 0:
+            aux_recv[plane] = aux_send[plane]
+            pl.semaphore_wait(barrier, 4 + dp_count - 1)
+        for step in range(1, dp_count):
+            other, device = at_plane(step)
+            send(
+                zsend.at[a, other],
+                zrecv.at[a, plane],
+                z_send_sem.at[a, step],
+                z_recv_sem.at[a, plane],
+                device,
+            )
+    for step in range(1, dp_count):
+        other, device = at_plane(step)
+        send(
+            aux_send.at[other],
+            aux_recv.at[plane],
+            aux_send_sem.at[step],
+            aux_recv_sem.at[plane],
+            device,
+        )
+
+    def shift_of(shape, axis):
+        slot = lax.broadcasted_iota(jnp.int32, shape, axis)
+        return slot, slot + (packed - CAP) * steps_of(slot, CAP, dp_count)
+
+    slot_index, slot_base = shift_of((slots, dp_count * packed), 0)
+    packed_index = lax.broadcasted_iota(jnp.int32, (slots, dp_count * packed), 1)
+    unpack = [
+        jnp.where(packed_index == slot_base + CAP * n, 1.0, 0.0).astype(BF16) for n in range(groups)
+    ]
+    for a in range(2):
+        for step in range(1, dp_count):
+            other = (plane + step) % dp_count
+            arrived(zrecv.at[a, other], z_send_sem.at[a, step], z_recv_sem.at[a, other])
+        received = zrecv[a].reshape(dp_count * packed, LANES)
+        for n in range(groups):
+            xbuf[a, h, :, n * LANES : (n + 1) * LANES] = dot(unpack[n], received, NN).astype(BF16)
+        for slot, partner in enumerate((hx, hy, sib)):
+            send(
+                xbuf.at[a, h],
+                xbuf.at[a, h],
+                x_send.at[a, slot],
+                x_recv.at[a, h],
+                at_hidden(partner),
+            )
+
+    def wait_x(a, index):
+        arrived(xbuf.at[a, index], x_send.at[a, 0], x_recv.at[a, index])
+
+    def forward(a, index, partner, slot):
+        send(
+            xbuf.at[a, index],
+            xbuf.at[a, index],
+            x_send.at[a, slot],
+            x_recv.at[a, index],
+            at_hidden(partner),
+        )
+
+    def project(which, index, start):
+        weight_copy(which, index).wait()
+        part = dot(xbuf[0 if which < 2 else 1, index], weights[which, index], NT)
+        acc[which] = part if start else acc[which] + part
+
+    def project_all(index):
+        for which in range(3):
+            project(which, index, False)
+
+    project(0, h, True)
+    project(1, h, True)
+    wait_x(0, hx)
+    forward(0, hx, hy, 3)
+    forward(0, hx, sib, 4)
+    wait_x(0, hy)
+    forward(0, hy, sib, 5)
+    project(2, h, True)
+    wait_x(1, hy)
+    forward(1, hy, hx, 3)
+    forward(1, hy, sib, 4)
+    wait_x(1, hx)
+    forward(1, hx, sib, 5)
+    wait_x(0, sib)
+    wait_x(1, sib)
+    project_all(sib)
+    project_all(hx)
+    wait_x(0, hd)
+    forward(0, hd, sib, 6)
+    wait_x(1, hd)
+    forward(1, hd, sib, 6)
+    project_all(hy)
+    for index in (hx + to_sib, hy + to_sib):
+        wait_x(0, index)
+        wait_x(1, index)
+        project_all(index)
+    project_all(hd)
+    wait_x(0, hd + to_sib)
+    wait_x(1, hd + to_sib)
+    project_all(hd + to_sib)
+    x_copy = pltpu.make_async_copy(xbuf.at[0], x_out, out_sem.at[0])
+    x_copy.start()
+
+    for step in range(1, dp_count):
+        other = (plane + step) % dp_count
+        arrived(aux_recv.at[other], aux_send_sem.at[step], aux_recv_sem.at[other])
+    slot_value = lax.broadcasted_iota(jnp.int32, (slots, rows), 0).astype(F32)
+    slot_prob = jnp.zeros((slots, 1), F32)
+    for source in range(dp_count):
+        source_rank = jnp.broadcast_to(aux_recv[source, 0:1, 0:rows], (slots, rows))
+        source_prob = jnp.broadcast_to(aux_recv[source, 1:2, 0:rows], (slots, rows))
+        hit = (source_rank >= 0.0) & (slot_value == source_rank + float(CAP * source))
+        slot_prob = slot_prob + jnp.sum(jnp.where(hit, source_prob, 0.0), axis=1, keepdims=True)
+
+    gate_pre = acc[0]
+    up_pre = acc[1]
+    back_pre = acc[2]
+    sigmoid_gate = jax.nn.sigmoid(gate_pre)
+    silu_gate = gate_pre * sigmoid_gate
+    scaled = slot_prob * back_pre
+    dbuf[0] = (scaled * up_pre * sigmoid_gate * (1.0 + gate_pre * (1.0 - sigmoid_gate))).astype(BF16)
+    dbuf[1] = (scaled * silu_gate).astype(BF16)
+    router = jnp.sum(silu_gate * up_pre * back_pre, axis=1, keepdims=True)
+    d_copy = pltpu.make_async_copy(dbuf, d_out, out_sem.at[1])
+    d_copy.start()
+
+    def row_of(column):
+        tall = jnp.concatenate(
+            [jnp.broadcast_to(column, (slots, LANES)), jnp.zeros((LANES - slots, LANES), F32)], axis=0
+        )
+        return tall.T[0:8, :]
+
+    q_send[0] = row_of(router)
+    send(q_send.at[0], q_recv.at[0], q_send_sem.at[0], q_recv_sem.at[0], at_hidden(sib))
+
+    def partial(index):
+        return dot(dbuf[0], weights[0, index], NN) + dot(dbuf[1], weights[1, index], NN)
+
+    for slot, index in enumerate((hd, hx, hy, h)):
+        one_send[slot] = partial(index + to_sib).astype(BF16)
+        send(
+            one_send.at[slot],
+            one_recv.at[slot],
+            one_send_sem.at[slot],
+            one_recv_sem.at[slot],
+            at_hidden(sib),
+        )
+    arrived(q_recv.at[0], q_send_sem.at[0], q_recv_sem.at[0])
+    q_send[1] = q_send[0] + q_recv[0]
+    for slot, index in enumerate((hd, hx, hy)):
+        send(
+            q_send.at[1],
+            q_recv.at[1 + slot],
+            q_send_sem.at[1 + slot],
+            q_recv_sem.at[1 + slot],
+            at_hidden(index),
+        )
+    for slot, index in enumerate((hd, hx, hy, h)):
+        own = partial(index)
+        arrived(one_recv.at[slot], one_send_sem.at[slot], one_recv_sem.at[slot])
+        total = own + one_recv[slot].astype(F32)
+        if slot == 3:
+            own_part[...] = total
+        else:
+            two_send[slot] = total.astype(BF16)
+            send(
+                two_send.at[slot],
+                two_recv.at[slot],
+                two_send_sem.at[slot],
+                two_recv_sem.at[slot],
+                at_hidden(index),
+            )
+
+    for slot in range(3):
+        arrived(q_recv.at[1 + slot], q_send_sem.at[1 + slot], q_recv_sem.at[1 + slot])
+    q_total = (q_send[1] + q_recv[2]) + (q_recv[3] + q_recv[1])
+    qz_send[...] = q_total
+    qz_recv[plane] = q_total
+    for step in range(1, dp_count):
+        _, device = at_plane(step)
+        send(qz_send, qz_recv.at[plane], qz_send_sem.at[step], qz_recv_sem.at[plane], device)
+
+    for slot in range(3):
+        arrived(two_recv.at[slot], two_send_sem.at[slot], two_recv_sem.at[slot])
+    features = (
+        own_part[...]
+        + two_recv[0].astype(F32)
+        + two_recv[1].astype(F32)
+        + two_recv[2].astype(F32)
+    ).astype(BF16)
+    _, slot_base = shift_of((dp_count * packed, slots), 1)
+    packed_index = lax.broadcasted_iota(jnp.int32, (dp_count * packed, slots), 0)
+    returned = jnp.zeros((dp_count * packed, LANES), F32)
+    for n in range(groups):
+        place = jnp.where(packed_index == slot_base + CAP * n, 1.0, 0.0).astype(BF16)
+        returned = returned + dot(place, features[:, n * LANES : (n + 1) * LANES], NN)
+    back_send[...] = returned.astype(BF16).reshape(dp_count, packed, LANES)
+    back_recv[plane] = back_send[plane]
+    for step in range(1, dp_count):
+        other, device = at_plane(step)
+        send(
+            back_send.at[other],
+            back_recv.at[plane],
+            back_send_sem.at[step],
+            back_recv_sem.at[plane],
+            device,
+        )
+
+    for step in range(1, dp_count):
+        other = (plane + step) % dp_count
+        arrived(qz_recv.at[other], qz_send_sem.at[step], qz_recv_sem.at[other])
+    q_rows = jnp.concatenate(
+        [qz_recv[j, 0:1, :] for j in range(dp_count)] + [jnp.zeros((LANES - dp_count, LANES), F32)],
+        axis=0,
+    )
+    q_columns = q_rows.T
+    wanted = lax.broadcasted_iota(jnp.int32, (LANES, rows), 0).astype(F32) - (CAP * plane).astype(F32)
+    found = [jnp.zeros((1, rows), F32), jnp.zeros((1, rows), F32)]
+    for j, owner in enumerate(owners):
+        hit = (wanted == jnp.broadcast_to(rank[j : j + 1, :], wanted.shape)) & (wanted >= 0.0)
+        column = jnp.broadcast_to(q_columns[:, j : j + 1], wanted.shape)
+        value = jnp.sum(jnp.where(hit, column, 0.0), axis=0, keepdims=True)
+        for k in range(2):
+            found[k] = found[k] + jnp.where(routes_ref[k : k + 1, :] == owner, value, 0.0)
+    grad_probs_ref[...] = jnp.concatenate(found, axis=0)
+
+    for step in range(1, dp_count):
+        other = (plane + step) % dp_count
+        arrived(back_recv.at[other], back_send_sem.at[step], back_recv_sem.at[other])
+    stacked = dot(select, back_recv[...].reshape(dp_count * packed, LANES), TN)
+    for n in range(groups):
+        grad_tokens_ref[:, n * LANES : (n + 1) * LANES] = stacked[n * rows : (n + 1) * rows, :].astype(
+            BF16
+        )
+
+    for copy in pending:
+        copy.wait_send()
+    x_copy.wait()
+    d_copy.wait()
+
+
+def outer_kernel(d_ref, x_ref, gate_ref, up_ref):
+    width = x_ref.shape[2]
+    for which, out in enumerate((gate_ref, up_ref)):
+        left = d_ref[which]
+        for index in range(x_ref.shape[0]):
+            out[:, index * width : (index + 1) * width] = dot(left, x_ref[index], TN).astype(BF16)
+
+
+def fused_body(dp_count, tokens, grad_out, routes, probs, gate_weight, up_weight, down_weight):
+    rows, width = tokens.shape
+    units, model = gate_weight.shape
+    hidden_count = model // width
+    groups = width // LANES
+    packed = CAP * groups
+    slots = CAP * dp_count
+    large_count = dp_count // 6
+    owners = tuple(j // 4 if j < 4 * large_count else j - 3 * large_count for j in range(dp_count))
+    dma = pltpu.SemaphoreType.DMA
+    vmem = pl.BlockSpec(memory_space=pltpu.VMEM)
+    anywhere = pl.BlockSpec(memory_space=pl.ANY)
+    grad_tokens, grad_probs, x_all, d_all = pl.pallas_call(
+        functools.partial(fused_kernel, dp_count, owners),
+        out_shape=(
+            jax.ShapeDtypeStruct((rows, width), BF16),
+            jax.ShapeDtypeStruct((2, rows), F32),
+            jax.ShapeDtypeStruct((hidden_count, slots, width), BF16),
+            jax.ShapeDtypeStruct((2, slots, units), BF16),
+        ),
+        in_specs=[vmem] * 4 + [anywhere] * 3,
+        out_specs=(vmem, vmem, anywhere, anywhere),
+        scratch_shapes=[
+            pltpu.VMEM((3, hidden_count, units, width), BF16),
+            dma((3, hidden_count)),
+            pltpu.VMEM((2, hidden_count, slots, width), BF16),
+            dma((2, 7)),
+            dma((2, hidden_count)),
+            pltpu.VMEM((2, dp_count, packed, LANES), BF16),
+            pltpu.VMEM((2, dp_count, packed, LANES), BF16),
+            dma((2, dp_count)),
+            dma((2, dp_count)),
+            pltpu.VMEM((dp_count, 8, LANES), F32),
+            pltpu.VMEM((dp_count, 8, LANES), F32),
+            dma((dp_count,)),
+            dma((dp_count,)),
+            pltpu.VMEM((3, slots, units), F32),
+            pltpu.VMEM((2, slots, units), BF16),
+            pltpu.VMEM((4, slots, width), BF16),
+            pltpu.VMEM((4, slots, width), BF16),
+            dma((4,)),
+            dma((4,)),
+            pltpu.VMEM((3, slots, width), BF16),
+            pltpu.VMEM((3, slots, width), BF16),
+            dma((3,)),
+            dma((3,)),
+            pltpu.VMEM((slots, width), F32),
+            pltpu.VMEM((2, 8, LANES), F32),
+            pltpu.VMEM((4, 8, LANES), F32),
+            dma((4,)),
+            dma((4,)),
+            pltpu.VMEM((dp_count, packed, LANES), BF16),
+            pltpu.VMEM((dp_count, packed, LANES), BF16),
+            dma((dp_count,)),
+            dma((dp_count,)),
+            pltpu.VMEM((8, LANES), F32),
+            pltpu.VMEM((dp_count, 8, LANES), F32),
+            dma((dp_count,)),
+            dma((dp_count,)),
+            dma((2,)),
+        ],
+        compiler_params=pltpu.CompilerParams(
+            collective_id=0, has_side_effects=True, vmem_limit_bytes=48 << 20
+        ),
+    )(routes.T, probs.T, tokens, grad_out, gate_weight, up_weight, down_weight)
+    tile = LANES
+    grad_gate, grad_up = pl.pallas_call(
+        outer_kernel,
+        grid=(units // tile,),
+        out_shape=(jax.ShapeDtypeStruct((units, model), BF16),) * 2,
+        in_specs=[
+            pl.BlockSpec((2, slots, tile), lambda i: (0, 0, i)),
+            pl.BlockSpec((hidden_count, slots, width), lambda i: (0, 0, 0)),
+        ],
+        out_specs=(pl.BlockSpec((tile, model), lambda i: (i, 0)),) * 2,
+        compiler_params=pltpu.CompilerParams(vmem_limit_bytes=32 << 20),
+    )(d_all, x_all)
+    return (grad_tokens, grad_probs.T, grad_gate, grad_up)
+
+
 def solution(mesh):
     placed = (
         P("dp", "hidden"),
@@ -106,8 +634,15 @@
         P(("dp", "hidden"), None),
         P(("dp", "hidden"), None),
     )
+
+    def local(tokens, grad_out, routes, probs, gate_weight, up_weight, down_weight):
+        args = (tokens, grad_out, routes, probs, gate_weight, up_weight, down_weight)
+        if fits(mesh.shape["dp"], mesh.shape["hidden"], tokens.shape, gate_weight.shape):
+            return fused_body(mesh.shape["dp"], *args)
+        return body(*args)
+
     return jax.shard_map(
-        body,
+        local,
         mesh=mesh,
         in_specs=placed,
         out_specs=(

time: 141 us -> 49.3 us (0.35)
  Pallas kernels: 0 us -> 44.4 us
  blocking collectives: 36.8 us -> 0 us
  matrix products: 34 us -> 0 us
  waiting for transfers between devices: 22.9 us -> 0 us
  starting transfers between devices: 22.6 us -> 0 us
  between operations: 14.2 us -> 0.65 us
  local copies, waits for them, and re-layouts: 6.82 us -> 4.02 us
  other arithmetic: 2.53 us -> 0 us
    pallas_call x0 -> x2, Pallas kernels: none -> 44.4 us  [the longest x1 37.3 us: fused_body(): pl.pallas_call(functools.partial(fused_kernel, dp_count, owners), out_sha...]
    dot_general x12 -> x0, matrix products: 34 us -> none  [the longest x1 6.23 us: body(): lax.dot_general(grad_up_pre, token_rows, over_rows, preferred_element_typ...]
    all_gather x2 -> x0, blocking collectives: 22.8 us -> none  [the longest x1 11.5 us: body(): lax.all_gather(recv_grads, 'hidden', axis=2, tiled=True)]
    all_to_all x5 -> x0, starting transfers between devices: 22.5 us -> none  [the longest x1 6.32 us: body(): lax.all_to_all(send_probs, 'dp', split_axis=0, concat_axis=0, tiled=True)]
    psum x1 -> x0, blocking collectives: 13.9 us -> none  [body(): router_payload = lax.psum(router_part, 'hidden')]
    reduce_scatter x1 -> x0, waiting for transfers between devices: 12.7 us -> none  [body(): lax.psum_scatter(lax.dot_general(gate_weight, grad_gate_pre, cross, prefe...]
    all_to_all x5 -> x0, waiting for transfers between devices: 10.2 us -> none  [the longest x1 4.6 us: body(): lax.all_to_all(send_probs, 'dp', split_axis=0, concat_axis=0, tiled=True)]
    reshape x3 -> x0, local copies, waits for them, and re-layouts: 5.84 us -> none  [the longest x1 2.13 us: body(): token_rows = full_tokens.reshape(row_count, full_tokens.shape[2])]
  transfers between devices with their start and end apart: 6 -> 0, of which waited for: 4 -> 0; matrix products, arithmetic and copies ran while one was open for 13% -> 0% of each run, Pallas kernels for 0% -> 0%
where the time goes in v1:
time: 49.3 us; the launch traced here: 49 us
  Pallas kernels  44.4 us (90%)
  local copies, waits for them, and re-layouts  4.02 us (8%)
  between operations  0.65 us (1%)
    pallas_call x1, Pallas kernels, fused_body(): pl.pallas_call(functools.partial(fused_kernel, dp_count, owners), out_sha...  37.3 us
    pallas_call x1, Pallas kernels, fused_body(): pl.pallas_call(outer_kernel, grid=(units // tile,), out_shape=(jax.ShapeD...  7.06 us
    unnamed x10, local copies, waits for them, and re-layouts  4.02 us

profile of v1, /device:TPU:0, one launch (start us, length us, event | category | flops | bytes accessed | tf_op | source)
XLA Modules:
  0.0 49.0 jit_solution(2061745278242414993)
XLA Ops:
  0.6 0.0 copy-start
  0.6 0.7 %copy-done = bf16[32,512]{1,0:T(8,128)(2,1)S(1)} copy-done((bf16[32,512]{1,0:T(8,128)(2,1)S(1)}, bf16[32,512]{1,0:T(8,128)(2,1)}, u32[]{:S(2)}) %copy-start) | copy-done | bytes 32792
  1.4 0.0 copy-start.1
  1.4 0.8 %copy-done.1 = bf16[32,512]{1,0:T(8,128)(2,1)S(1)} copy-done((bf16[32,512]{1,0:T(8,128)(2,1)S(1)}, bf16[32,512]{1,0:T(8,128)(2,1)}, u32[]{:S(2)}) %copy-start.1) | copy-done | bytes 32792
  2.2 0.0 copy-start.2
  2.2 0.7 %copy-done.2 = s32[32,2]{0,1:T(2,128)S(1)} copy-done((s32[32,2]{0,1:T(2,128)S(1)}, s32[32,2]{0,1:T(2,128)}, u32[]{:S(2)}) %copy-start.2) | copy-done | bytes 280
  2.8 0.0 copy-start.3
  2.8 0.7 %copy-done.3 = bf16[32,2]{0,1:T(2,128)(2,1)S(1)} copy-done((bf16[32,2]{0,1:T(2,128)(2,1)S(1)}, bf16[32,2]{0,1:T(2,128)(2,1)}, u32[]{:S(2)}) %copy-start.3) | copy-done | bytes 152
  3.5 37.3 %shard_map.102 = (bf16[32,512]{1,0:T(8,128)(2,1)S(1)}, f32[2,32]{1,0:T(2,128)S(1)}, bf16[8,80,512]{2,1,0:T(8,128)(2,1)S(1)}, bf16[2,80,896]{2,1,0:T(8,128)(2,1)S(1)}) custom-call(s32[2,32]{1,0:T(2,128)S(1)} %bitcast.3, bf16[2,32]{1,0:T(2,128)(2,1)S(1)} %bitcast.5, bf16[32,512]{1,0:T(8,128)(2,1)S(1)} %copy-done, bf16[32,512]{1,0:T(8,128)(2,1)S(1)} %copy-done.1, ...), custom_call_target="tpu_custom_call" | custom-call | tf_op jit(solution)/shard_map/pallas_call | solution.py:559
  40.8 7.1 %shard_map.103 = (bf16[896,4096]{1,0:T(8,128)(2,1)}, bf16[896,4096]{1,0:T(8,128)(2,1)}) custom-call(bf16[2,80,896]{2,1,0:T(8,128)(2,1)S(1)} %get-tuple-element.12.d_ref, bf16[8,80,512]{2,1,0:T(8,128)(2,1)S(1)} %get-tuple-element.13.x_ref), custom_call_target="tpu_custom_call" | custom-call | tf_op jit(solution)/shard_map/pallas_call | solution.py:613
  47.9 0.6 %copy.13 = bf16[32,512]{1,0:T(8,128)(2,1)} copy(bf16[32,512]{1,0:T(8,128)(2,1)S(1)} %get-tuple-element.20) | data formatting | bytes 65536
  48.5 0.6 %copy.14 = f32[32,2]{0,1:T(2,128)} copy(f32[32,2]{0,1:T(2,128)S(1)} %bitcast.4) | data formatting | bytes 512
Async XLA Ops:
  0.6 0.8 %copy-start = (bf16[32,512]{1,0:T(8,128)(2,1)S(1)}, bf16[32,512]{1,0:T(8,128)(2,1)}, u32[]{:S(2)}) copy-start(bf16[32,512]{1,0:T(8,128)(2,1)} %tokens_ref.1) | copy-start | bytes 98308
  1.4 0.8 %copy-start.1 = (bf16[32,512]{1,0:T(8,128)(2,1)S(1)}, bf16[32,512]{1,0:T(8,128)(2,1)}, u32[]{:S(2)}) copy-start(bf16[32,512]{1,0:T(8,128)(2,1)} %grads_ref.1) | copy-start | bytes 98308
  2.2 0.7 %copy-start.2 = (s32[32,2]{0,1:T(2,128)S(1)}, s32[32,2]{0,1:T(2,128)}, u32[]{:S(2)}) copy-start(s32[32,2]{0,1:T(2,128)} %param.9) | copy-start | bytes 772
  2.8 0.7 %copy-start.3 = (bf16[32,2]{0,1:T(2,128)(2,1)S(1)}, bf16[32,2]{0,1:T(2,128)(2,1)}, u32[]{:S(2)}) copy-start(bf16[32,2]{0,1:T(2,128)(2,1)} %param.10) | copy-start | bytes 388

commit v2 on v1

--- a/solution.py
+++ b/solution.py
@@ -138,10 +138,10 @@
 def fused_kernel(
     dp_count,
     owners,
-    routes_ref,
-    probs_ref,
-    tokens_ref,
-    grads_ref,
+    routes_hbm,
+    probs_hbm,
+    tokens_hbm,
+    grads_hbm,
     gate_hbm,
     up_hbm,
     down_hbm,
@@ -163,6 +163,7 @@
     aux_send_sem,
     aux_recv_sem,
     acc,
+    tbuf,
     dbuf,
     one_send,
     one_recv,
@@ -186,6 +187,11 @@
     qz_send_sem,
     qz_recv_sem,
     out_sem,
+    routes_ref,
+    probs_ref,
+    tokens_ref,
+    grads_ref,
+    in_sem,
 ):
     rows, width = tokens_ref.shape
     groups = width // LANES
@@ -209,6 +215,20 @@
         other = (plane + step) % dp_count
         return other, (other, h)
 
+    inputs = [
+        pltpu.make_async_copy(source, target, in_sem.at[n])
+        for n, (source, target) in enumerate(
+            (
+                (routes_hbm, routes_ref),
+                (probs_hbm, probs_ref),
+                (tokens_hbm, tokens_ref),
+                (grads_hbm, grads_ref),
+            )
+        )
+    ]
+    for copy in inputs:
+        copy.start()
+
     barrier = pltpu.get_barrier_semaphore()
     for index in (sib, hx, hy, hd):
         pl.semaphore_signal(barrier, inc=1, device_id=at_hidden(index), device_id_type=MESH)
@@ -224,9 +244,10 @@
             source.at[:, columns], weights.at[which, index], weight_sem.at[which, index]
         )
 
-    for index in order:
-        for which in range(3):
-            weight_copy(which, index).start()
+    def fetch_weights(indices):
+        for index in indices:
+            for which in range(3):
+                weight_copy(which, index).start()
 
     pending = []
 
@@ -256,6 +277,8 @@
     owner_of = jnp.full((8, rows), -1, jnp.int32)
     for j, owner in enumerate(owners):
         owner_of = jnp.where(block_row == j, owner, owner_of)
+    inputs[0].wait()
+    inputs[1].wait()
     first = jnp.broadcast_to(routes_ref[0:1, :], (8, rows))
     second = jnp.broadcast_to(routes_ref[1:2, :], (8, rows))
     prob_rows = probs_ref[...].astype(F32)
@@ -292,6 +315,7 @@
     ).astype(BF16)
 
     for a, ref in enumerate((tokens_ref, grads_ref)):
+        inputs[2 + a].wait()
         stacked = jnp.concatenate(
             [ref[:, n * LANES : (n + 1) * LANES] for n in range(groups)], axis=0
         )
@@ -319,6 +343,8 @@
             device,
         )
 
+    fetch_weights(order[:4])
+
     def shift_of(shape, axis):
         slot = lax.broadcasted_iota(jnp.int32, shape, axis)
         return slot, slot + (packed - CAP) * steps_of(slot, CAP, dp_count)
@@ -344,6 +370,8 @@
                 at_hidden(partner),
             )
 
+    fetch_weights(order[4:6])
+
     def wait_x(a, index):
         arrived(xbuf.at[a, index], x_send.at[a, 0], x_recv.at[a, index])
 
@@ -358,7 +386,7 @@
 
     def project(which, index, start):
         weight_copy(which, index).wait()
-        part = dot(xbuf[0 if which < 2 else 1, index], weights[which, index], NT)
+        part = dot(weights[which, index], xbuf[0 if which < 2 else 1, index], NT)
         acc[which] = part if start else acc[which] + part
 
     def project_all(index):
@@ -378,6 +406,7 @@
     forward(1, hy, sib, 4)
     wait_x(1, hx)
     forward(1, hx, sib, 5)
+    fetch_weights(order[6:])
     wait_x(0, sib)
     wait_x(1, sib)
     project_all(sib)
@@ -409,32 +438,36 @@
         hit = (source_rank >= 0.0) & (slot_value == source_rank + float(CAP * source))
         slot_prob = slot_prob + jnp.sum(jnp.where(hit, source_prob, 0.0), axis=1, keepdims=True)
 
+    def tall(values, count):
+        gap = jnp.zeros((LANES - count, values.shape[1]), F32)
+        return jnp.concatenate([values, gap], axis=0) if count < LANES else values
+
+    prob_row = tall(jnp.broadcast_to(slot_prob, (slots, LANES)), slots).T[0:1, 0:slots]
     gate_pre = acc[0]
     up_pre = acc[1]
     back_pre = acc[2]
     sigmoid_gate = jax.nn.sigmoid(gate_pre)
     silu_gate = gate_pre * sigmoid_gate
-    scaled = slot_prob * back_pre
-    dbuf[0] = (scaled * up_pre * sigmoid_gate * (1.0 + gate_pre * (1.0 - sigmoid_gate))).astype(BF16)
-    dbuf[1] = (scaled * silu_gate).astype(BF16)
-    router = jnp.sum(silu_gate * up_pre * back_pre, axis=1, keepdims=True)
-    d_copy = pltpu.make_async_copy(dbuf, d_out, out_sem.at[1])
+    scaled = prob_row * back_pre
+    grad_gate_pre = scaled * up_pre * sigmoid_gate * (1.0 + gate_pre * (1.0 - sigmoid_gate))
+    grad_up_pre = scaled * silu_gate
+    for which, value in enumerate((grad_gate_pre, grad_up_pre)):
+        tbuf[which] = value.astype(BF16)
+        dbuf[which] = value.T.astype(BF16)
+    router = jnp.sum(silu_gate * up_pre * back_pre, axis=0, keepdims=True)
+    d_copy = pltpu.make_async_copy(tbuf, d_out, out_sem.at[1])
     d_copy.start()
-
-    def row_of(column):
-        tall = jnp.concatenate(
-            [jnp.broadcast_to(column, (slots, LANES)), jnp.zeros((LANES - slots, LANES), F32)], axis=0
-        )
-        return tall.T[0:8, :]
-
-    q_send[0] = row_of(router)
+    q_send[0] = jnp.zeros((8, LANES), F32)
+    q_send[0, 0:1, 0:slots] = router
     send(q_send.at[0], q_recv.at[0], q_send_sem.at[0], q_recv_sem.at[0], at_hidden(sib))
 
     def partial(index):
         return dot(dbuf[0], weights[0, index], NN) + dot(dbuf[1], weights[1, index], NN)
 
-    for slot, index in enumerate((hd, hx, hy, h)):
-        one_send[slot] = partial(index + to_sib).astype(BF16)
+    chips = (hd, hx, hy, h)
+
+    def sibling_part(slot):
+        one_send[slot] = partial(chips[slot] + to_sib).astype(BF16)
         send(
             one_send.at[slot],
             one_recv.at[slot],
@@ -442,6 +475,8 @@
             one_recv_sem.at[slot],
             at_hidden(sib),
         )
+
+    sibling_part(0)
     arrived(q_recv.at[0], q_send_sem.at[0], q_recv_sem.at[0])
     q_send[1] = q_send[0] + q_recv[0]
     for slot, index in enumerate((hd, hx, hy)):
@@ -452,7 +487,9 @@
             q_recv_sem.at[1 + slot],
             at_hidden(index),
         )
-    for slot, index in enumerate((hd, hx, hy, h)):
+    for slot, index in enumerate(chips):
+        if slot < 3:
+            sibling_part(slot + 1)
         own = partial(index)
         arrived(one_recv.at[slot], one_send_sem.at[slot], one_recv_sem.at[slot])
         total = own + one_recv[slot].astype(F32)
@@ -536,12 +573,14 @@
     d_copy.wait()
 
 
-def outer_kernel(d_ref, x_ref, gate_ref, up_ref):
-    width = x_ref.shape[2]
-    for which, out in enumerate((gate_ref, up_ref)):
-        left = d_ref[which]
-        for index in range(x_ref.shape[0]):
-            out[:, index * width : (index + 1) * width] = dot(left, x_ref[index], TN).astype(BF16)
+def outer_kernel(d_ref, x_ref, tokens_ref, probs_ref, gate_ref, up_ref, tokens_out, probs_out):
+    gate_ref[...] = dot(d_ref[0], x_ref[0], NN).astype(BF16)
+    up_ref[...] = dot(d_ref[1], x_ref[0], NN).astype(BF16)
+
+    @pl.when(pl.program_id(0) == 0)
+    def _():
+        tokens_out[...] = tokens_ref[...]
+        probs_out[...] = probs_ref[...]
 
 
 def fused_body(dp_count, tokens, grad_out, routes, probs, gate_weight, up_weight, down_weight):
@@ -562,9 +601,9 @@
             jax.ShapeDtypeStruct((rows, width), BF16),
             jax.ShapeDtypeStruct((2, rows), F32),
             jax.ShapeDtypeStruct((hidden_count, slots, width), BF16),
-            jax.ShapeDtypeStruct((2, slots, units), BF16),
+            jax.ShapeDtypeStruct((2, units, slots), BF16),
         ),
-        in_specs=[vmem] * 4 + [anywhere] * 3,
+        in_specs=[pl.BlockSpec(memory_space=pltpu.HBM)] * 7,
         out_specs=(vmem, vmem, anywhere, anywhere),
         scratch_shapes=[
             pltpu.VMEM((3, hidden_count, units, width), BF16),
@@ -580,7 +619,8 @@
             pltpu.VMEM((dp_count, 8, LANES), F32),
             dma((dp_count,)),
             dma((dp_count,)),
-            pltpu.VMEM((3, slots, units), F32),
+            pltpu.VMEM((3, units, slots), F32),
+            pltpu.VMEM((2, units, slots), BF16),
             pltpu.VMEM((2, slots, units), BF16),
             pltpu.VMEM((4, slots, width), BF16),
             pltpu.VMEM((4, slots, width), BF16),
@@ -604,23 +644,39 @@
             dma((dp_count,)),
             dma((dp_count,)),
             dma((2,)),
+            pltpu.VMEM((2, rows), jnp.int32),
+            pltpu.VMEM((2, rows), BF16),
+            pltpu.VMEM((rows, width), BF16),
+            pltpu.VMEM((rows, width), BF16),
+            dma((4,)),
         ],
         compiler_params=pltpu.CompilerParams(
-            collective_id=0, has_side_effects=True, vmem_limit_bytes=48 << 20
+            collective_id=0, has_side_effects=True, vmem_limit_bytes=64 << 20
         ),
     )(routes.T, probs.T, tokens, grad_out, gate_weight, up_weight, down_weight)
-    tile = LANES
-    grad_gate, grad_up = pl.pallas_call(
+    grad_gate, grad_up, grad_tokens, grad_probs = pl.pallas_call(
         outer_kernel,
-        grid=(units // tile,),
-        out_shape=(jax.ShapeDtypeStruct((units, model), BF16),) * 2,
+        grid=(hidden_count,),
+        out_shape=(
+            jax.ShapeDtypeStruct((units, model), BF16),
+            jax.ShapeDtypeStruct((units, model), BF16),
+            jax.ShapeDtypeStruct((rows, width), BF16),
+            jax.ShapeDtypeStruct((2, rows), F32),
+        ),
         in_specs=[
-            pl.BlockSpec((2, slots, tile), lambda i: (0, 0, i)),
-            pl.BlockSpec((hidden_count, slots, width), lambda i: (0, 0, 0)),
+            pl.BlockSpec((2, units, slots), lambda i: (0, 0, 0)),
+            pl.BlockSpec((1, slots, width), lambda i: (i, 0, 0)),
+            pl.BlockSpec((rows, width), lambda i: (0, 0)),
+            pl.BlockSpec((2, rows), lambda i: (0, 0)),
         ],
-        out_specs=(pl.BlockSpec((tile, model), lambda i: (i, 0)),) * 2,
-        compiler_params=pltpu.CompilerParams(vmem_limit_bytes=32 << 20),
-    )(d_all, x_all)
+        out_specs=(
+            pl.BlockSpec((units, width), lambda i: (0, i)),
+            pl.BlockSpec((units, width), lambda i: (0, i)),
+            pl.BlockSpec((rows, width), lambda i: (0, 0)),
+            pl.BlockSpec((2, rows), lambda i: (0, 0)),
+        ),
+        compiler_params=pltpu.CompilerParams(vmem_limit_bytes=64 << 20),
+    )(d_all, x_all, grad_tokens, grad_probs)
     return (grad_tokens, grad_probs.T, grad_gate, grad_up)
 
 

time: 49.3 us -> 49.2 us (level)
  local copies, waits for them, and re-layouts: 4.02 us -> 0 us
  Pallas kernels: 44.4 us -> 48.2 us
    unnamed x10 -> x0, local copies, waits for them, and re-layouts: 4.02 us -> none
    pallas_call x1, Pallas kernels: 7.06 us -> 9.42 us  [fused_body(): pl.pallas_call(outer_kernel, grid=(hidden_count,), out_shape=(jax.ShapeDt...]
    pallas_call x1, Pallas kernels: 37.3 us -> 38.8 us  [fused_body(): pl.pallas_call(functools.partial(fused_kernel, dp_count, owners), out_sha...]
where the time goes in v2:
time: 49.2 us; the launch traced here: 48.8 us
  Pallas kernels  48.2 us (98%)
  between operations  0.64 us (1%)
    pallas_call x1, Pallas kernels, fused_body(): pl.pallas_call(functools.partial(fused_kernel, dp_count, owners), out_sha...  38.8 us
    pallas_call x1, Pallas kernels, fused_body(): pl.pallas_call(outer_kernel, grid=(hidden_count,), out_shape=(jax.ShapeDt...  9.42 us

profile of v2, /device:TPU:0, one launch (start us, length us, event | category | flops | bytes accessed | tf_op | source)
XLA Modules:
  0.0 48.8 jit_solution(11338636627776585213)
XLA Ops:
  0.6 38.8 %shard_map.102 = (bf16[32,512]{1,0:T(8,128)(2,1)}, f32[2,32]{1,0:T(2,128)}, bf16[8,80,512]{2,1,0:T(8,128)(2,1)}, bf16[2,896,80]{2,1,0:T(8,128)(2,1)}) custom-call(s32[2,32]{1,0:T(2,128)} %bitcast.3, bf16[2,32]{1,0:T(2,128)(2,1)} %bitcast.4, bf16[32,512]{1,0:T(8,128)(2,1)} %tokens_hbm.1, bf16[32,512]{1,0:T(8,128)(2,1)} %grads_hbm.1, ...), custom_call_target="tpu_custom_call" | custom-call | tf_op jit(solution)/shard_map/pallas_call | solution.py:598
  39.4 9.4 %shard_map.103 = (bf16[896,4096]{1,0:T(8,128)(2,1)}, bf16[896,4096]{1,0:T(8,128)(2,1)}, bf16[32,512]{1,0:T(8,128)(2,1)}, f32[2,32]{1,0:T(2,128)}) custom-call(bf16[2,896,80]{2,1,0:T(8,128)(2,1)} %get-tuple-element.12.d_ref, bf16[8,80,512]{2,1,0:T(8,128)(2,1)} %get-tuple-element.13.x_ref, bf16[32,512]{1,0:T(8,128)(2,1)} %get-tuple-element.14.tokens_ref, ...), custom_call_target="tpu_custom_call" | custom-call | tf_op jit(solution)/shard_map/pallas_call | solution.py:657

commit v3 on v2

--- a/solution.py
+++ b/solution.py
@@ -128,6 +128,10 @@
     return lax.dot_general(a, b, dims, preferred_element_type=F32)
 
 
+def strips(total, size):
+    return [(start, min(size, total - start)) for start in range(0, total, size)]
+
+
 def steps_of(values, size, count):
     total = jnp.zeros_like(values)
     for edge in range(1, count):
@@ -163,7 +167,6 @@
     aux_send_sem,
     aux_recv_sem,
     acc,
-    tbuf,
     dbuf,
     one_send,
     one_recv,
@@ -194,6 +197,7 @@
     in_sem,
 ):
     rows, width = tokens_ref.shape
+    units = gate_hbm.shape[0]
     groups = width // LANES
     packed = CAP * groups
     slots = CAP * dp_count
@@ -249,6 +253,7 @@
             for which in range(3):
                 weight_copy(which, index).start()
 
+    fetch_weights(order[:2])
     pending = []
 
     def send(source, target, send_sem, recv_sem, device):
@@ -343,7 +348,7 @@
             device,
         )
 
-    fetch_weights(order[:4])
+    fetch_weights(order[2:6])
 
     def shift_of(shape, axis):
         slot = lax.broadcasted_iota(jnp.int32, shape, axis)
@@ -370,7 +375,7 @@
                 at_hidden(partner),
             )
 
-    fetch_weights(order[4:6])
+    fetch_weights(order[6:])
 
     def wait_x(a, index):
         arrived(xbuf.at[a, index], x_send.at[a, 0], x_recv.at[a, index])
@@ -386,8 +391,12 @@
 
     def project(which, index, start):
         weight_copy(which, index).wait()
-        part = dot(weights[which, index], xbuf[0 if which < 2 else 1, index], NT)
-        acc[which] = part if start else acc[which] + part
+        left = xbuf[0 if which < 2 else 1, index]
+        for begin, size in strips(units, 2 * LANES):
+            part = dot(left, weights[which, index, begin : begin + size, :], NT)
+            if not start:
+                part = part + acc[which, :, begin : begin + size]
+            acc[which, :, begin : begin + size] = part
 
     def project_all(index):
         for which in range(3):
@@ -406,7 +415,6 @@
     forward(1, hy, sib, 4)
     wait_x(1, hx)
     forward(1, hx, sib, 5)
-    fetch_weights(order[6:])
     wait_x(0, sib)
     wait_x(1, sib)
     project_all(sib)
@@ -438,36 +446,44 @@
         hit = (source_rank >= 0.0) & (slot_value == source_rank + float(CAP * source))
         slot_prob = slot_prob + jnp.sum(jnp.where(hit, source_prob, 0.0), axis=1, keepdims=True)
 
-    def tall(values, count):
-        gap = jnp.zeros((LANES - count, values.shape[1]), F32)
-        return jnp.concatenate([values, gap], axis=0) if count < LANES else values
-
-    prob_row = tall(jnp.broadcast_to(slot_prob, (slots, LANES)), slots).T[0:1, 0:slots]
-    gate_pre = acc[0]
-    up_pre = acc[1]
-    back_pre = acc[2]
-    sigmoid_gate = jax.nn.sigmoid(gate_pre)
-    silu_gate = gate_pre * sigmoid_gate
-    scaled = prob_row * back_pre
-    grad_gate_pre = scaled * up_pre * sigmoid_gate * (1.0 + gate_pre * (1.0 - sigmoid_gate))
-    grad_up_pre = scaled * silu_gate
-    for which, value in enumerate((grad_gate_pre, grad_up_pre)):
-        tbuf[which] = value.astype(BF16)
-        dbuf[which] = value.T.astype(BF16)
-    router = jnp.sum(silu_gate * up_pre * back_pre, axis=0, keepdims=True)
-    d_copy = pltpu.make_async_copy(tbuf, d_out, out_sem.at[1])
+    router = jnp.zeros((slots, LANES), F32)
+    slot_prob = jnp.broadcast_to(slot_prob, (slots, LANES))
+    for begin, size in strips(units, LANES):
+        part = slice(begin, begin + size)
+        gate_pre = acc[0, :, part]
+        up_pre = acc[1, :, part]
+        back_pre = acc[2, :, part]
+        sigmoid_gate = jax.nn.sigmoid(gate_pre)
+        silu_gate = gate_pre * sigmoid_gate
+        scaled = slot_prob * back_pre
+        dbuf[0, :, part] = (
+            scaled * up_pre * sigmoid_gate * (1.0 + gate_pre * (1.0 - sigmoid_gate))
+        ).astype(BF16)
+        dbuf[1, :, part] = (scaled * silu_gate).astype(BF16)
+        router = router + silu_gate * up_pre * back_pre
+    d_copy = pltpu.make_async_copy(dbuf, d_out, out_sem.at[1])
     d_copy.start()
-    q_send[0] = jnp.zeros((8, LANES), F32)
-    q_send[0, 0:1, 0:slots] = router
+    router = jnp.broadcast_to(jnp.sum(router, axis=1, keepdims=True), (slots, LANES))
+    if slots < LANES:
+        router = jnp.concatenate([router, jnp.zeros((LANES - slots, LANES), F32)], axis=0)
+    q_send[0] = router.T[0:8, :]
     send(q_send.at[0], q_recv.at[0], q_send_sem.at[0], q_recv_sem.at[0], at_hidden(sib))
 
-    def partial(index):
-        return dot(dbuf[0], weights[0, index], NN) + dot(dbuf[1], weights[1, index], NN)
+    column_strips = strips(width, 2 * LANES)
+
+    def partial(index, begin, size):
+        part = slice(begin, begin + size)
+        return dot(dbuf[0], weights[0, index, :, part], NN) + dot(
+            dbuf[1], weights[1, index, :, part], NN
+        )
 
     chips = (hd, hx, hy, h)
 
     def sibling_part(slot):
-        one_send[slot] = partial(chips[slot] + to_sib).astype(BF16)
+        for begin, size in column_strips:
+            one_send[slot, :, begin : begin + size] = partial(
+                chips[slot] + to_sib, begin, size
+            ).astype(BF16)
         send(
             one_send.at[slot],
             one_recv.at[slot],
@@ -490,9 +506,10 @@
     for slot, index in enumerate(chips):
         if slot < 3:
             sibling_part(slot + 1)
-        own = partial(index)
+        for begin, size in column_strips:
+            own_part[:, begin : begin + size] = partial(index, begin, size)
         arrived(one_recv.at[slot], one_send_sem.at[slot], one_recv_sem.at[slot])
-        total = own + one_recv[slot].astype(F32)
+        total = own_part[...] + one_recv[slot].astype(F32)
         if slot == 3:
             own_part[...] = total
         else:
@@ -574,8 +591,15 @@
 
 
 def outer_kernel(d_ref, x_ref, tokens_ref, probs_ref, gate_ref, up_ref, tokens_out, probs_out):
-    gate_ref[...] = dot(d_ref[0], x_ref[0], NN).astype(BF16)
-    up_ref[...] = dot(d_ref[1], x_ref[0], NN).astype(BF16)
+    width = x_ref.shape[2]
+    for which, out in enumerate((gate_ref, up_ref)):
+        left = d_ref[which].astype(F32).T.astype(BF16)
+        for index in range(x_ref.shape[0]):
+            for begin, size in strips(width, 2 * LANES):
+                start = index * width + begin
+                out[:, start : start + size] = dot(
+                    left, x_ref[index, :, begin : begin + size], NN
+                ).astype(BF16)
 
     @pl.when(pl.program_id(0) == 0)
     def _():
@@ -601,7 +625,7 @@
             jax.ShapeDtypeStruct((rows, width), BF16),
             jax.ShapeDtypeStruct((2, rows), F32),
             jax.ShapeDtypeStruct((hidden_count, slots, width), BF16),
-            jax.ShapeDtypeStruct((2, units, slots), BF16),
+            jax.ShapeDtypeStruct((2, slots, units), BF16),
         ),
         in_specs=[pl.BlockSpec(memory_space=pltpu.HBM)] * 7,
         out_specs=(vmem, vmem, anywhere, anywhere),
@@ -619,8 +643,7 @@
             pltpu.VMEM((dp_count, 8, LANES), F32),
             dma((dp_count,)),
             dma((dp_count,)),
-            pltpu.VMEM((3, units, slots), F32),
-            pltpu.VMEM((2, units, slots), BF16),
+            pltpu.VMEM((3, slots, units), F32),
             pltpu.VMEM((2, slots, units), BF16),
             pltpu.VMEM((4, slots, width), BF16),
             pltpu.VMEM((4, slots, width), BF16),
@@ -656,7 +679,7 @@
     )(routes.T, probs.T, tokens, grad_out, gate_weight, up_weight, down_weight)
     grad_gate, grad_up, grad_tokens, grad_probs = pl.pallas_call(
         outer_kernel,
-        grid=(hidden_count,),
+        grid=(units // LANES,),
         out_shape=(
             jax.ShapeDtypeStruct((units, model), BF16),
             jax.ShapeDtypeStruct((units, model), BF16),
@@ -664,14 +687,14 @@
             jax.ShapeDtypeStruct((2, rows), F32),
         ),
         in_specs=[
-            pl.BlockSpec((2, units, slots), lambda i: (0, 0, 0)),
-            pl.BlockSpec((1, slots, width), lambda i: (i, 0, 0)),
+            pl.BlockSpec((2, slots, LANES), lambda i: (0, 0, i)),
+            pl.BlockSpec((hidden_count, slots, width), lambda i: (0, 0, 0)),
             pl.BlockSpec((rows, width), lambda i: (0, 0)),
             pl.BlockSpec((2, rows), lambda i: (0, 0)),
         ],
         out_specs=(
-            pl.BlockSpec((units, width), lambda i: (0, i)),
-            pl.BlockSpec((units, width), lambda i: (0, i)),
+            pl.BlockSpec((LANES, model), lambda i: (i, 0)),
+            pl.BlockSpec((LANES, model), lambda i: (i, 0)),
             pl.BlockSpec((rows, width), lambda i: (0, 0)),
             pl.BlockSpec((2, rows), lambda i: (0, 0)),
         ),

time: 49.2 us -> 48.2 us (0.980)
  Pallas kernels: 48.2 us -> 47.2 us
    pallas_call x1, Pallas kernels: 38.8 us -> 37.9 us  [fused_body(): pl.pallas_call(functools.partial(fused_kernel, dp_count, owners), out_sha...]
where the time goes in v3:
time: 48.2 us; the launch traced here: 47.9 us
  Pallas kernels  47.2 us (98%)
  between operations  0.64 us (1%)
    pallas_call x1, Pallas kernels, fused_body(): pl.pallas_call(functools.partial(fused_kernel, dp_count, owners), out_sha...  37.9 us
    pallas_call x1, Pallas kernels, fused_body(): pl.pallas_call(outer_kernel, grid=(units // LANES,), out_shape=(jax.Shape...  9.32 us

profile of v3, /device:TPU:0, one launch (start us, length us, event | category | flops | bytes accessed | tf_op | source)
XLA Modules:
  0.0 47.9 jit_solution(7975510712848007721)
XLA Ops:
  0.6 37.9 %shard_map.102 = (bf16[32,512]{1,0:T(8,128)(2,1)}, f32[2,32]{1,0:T(2,128)}, bf16[8,80,512]{2,1,0:T(8,128)(2,1)}, bf16[2,80,896]{2,1,0:T(8,128)(2,1)}) custom-call(s32[2,32]{1,0:T(2,128)} %bitcast.3, bf16[2,32]{1,0:T(2,128)(2,1)} %bitcast.4, bf16[32,512]{1,0:T(8,128)(2,1)} %tokens_hbm.1, bf16[32,512]{1,0:T(8,128)(2,1)} %grads_hbm.1, ...), custom_call_target="tpu_custom_call" | custom-call | tf_op jit(solution)/shard_map/pallas_call | solution.py:622
  38.5 9.3 %shard_map.103 = (bf16[896,4096]{1,0:T(8,128)(2,1)}, bf16[896,4096]{1,0:T(8,128)(2,1)}, bf16[32,512]{1,0:T(8,128)(2,1)}, f32[2,32]{1,0:T(2,128)}) custom-call(bf16[2,80,896]{2,1,0:T(8,128)(2,1)} %get-tuple-element.12.d_ref, bf16[8,80,512]{2,1,0:T(8,128)(2,1)} %get-tuple-element.13.x_ref, bf16[32,512]{1,0:T(8,128)(2,1)} %get-tuple-element.14.tokens_ref, ...), custom_call_target="tpu_custom_call" | custom-call | tf_op jit(solution)/shard_map/pallas_call | solution.py:680

commit v4 on v3

--- a/solution.py
+++ b/solution.py
@@ -167,6 +167,7 @@
     aux_send_sem,
     aux_recv_sem,
     acc,
+    router_sum,
     dbuf,
     one_send,
     one_recv,
@@ -212,6 +213,9 @@
     hy = h + 4 - 8 * y_pos
     hd = hx + 4 - 8 * y_pos
 
+    def chip_at(flip_x, flip_y):
+        return h + flip_x * (2 - 4 * x_pos) + flip_y * (4 - 8 * y_pos)
+
     def at_hidden(index):
         return (plane, index)
 
@@ -239,7 +243,7 @@
     for step in range(1, dp_count):
         pl.semaphore_signal(barrier, inc=1, device_id=at_plane(step)[1], device_id_type=MESH)
 
-    order = (h, sib, hx, hy, hx + to_sib, hy + to_sib, hd, hd + to_sib)
+    order = (h, sib, hx, hx + to_sib, hy, hy + to_sib, hd, hd + to_sib)
 
     def weight_copy(which, index):
         columns = pl.ds(pl.multiple_of(index * width, width), width)
@@ -256,17 +260,19 @@
     fetch_weights(order[:2])
     pending = []
 
-    def send(source, target, send_sem, recv_sem, device):
-        copy = pltpu.make_async_remote_copy(
+    def start(source, target, send_sem, recv_sem, device):
+        pltpu.make_async_remote_copy(
             src_ref=source,
             dst_ref=target,
             send_sem=send_sem,
             recv_sem=recv_sem,
             device_id=device,
             device_id_type=MESH,
-        )
-        copy.start()
-        pending.append(copy)
+        ).start()
+
+    def send(source, target, send_sem, recv_sem, device):
+        start(source, target, send_sem, recv_sem, device)
+        pending.append((source, send_sem))
 
     def arrived(target, send_sem, recv_sem):
         pltpu.make_async_remote_copy(
@@ -381,7 +387,7 @@
         arrived(xbuf.at[a, index], x_send.at[a, 0], x_recv.at[a, index])
 
     def forward(a, index, partner, slot):
-        send(
+        start(
             xbuf.at[a, index],
             xbuf.at[a, index],
             x_send.at[a, slot],
@@ -389,49 +395,56 @@
             at_hidden(partner),
         )
 
-    def project(which, index, start):
-        weight_copy(which, index).wait()
-        left = xbuf[0 if which < 2 else 1, index]
-        for begin, size in strips(units, 2 * LANES):
-            part = dot(left, weights[which, index, begin : begin + size, :], NT)
-            if not start:
-                part = part + acc[which, :, begin : begin + size]
-            acc[which, :, begin : begin + size] = part
-
-    def project_all(index):
+    acc[...] = jnp.zeros_like(acc)
+
+    @pl.loop(0, 8)
+    def _(i):
+        @pl.when(i == 1)
+        def _():
+            wait_x(0, hx)
+            forward(0, hx, hy, 3)
+            forward(0, hx, sib, 4)
+            wait_x(0, hy)
+            forward(0, hy, sib, 5)
+            wait_x(0, sib)
+            wait_x(1, sib)
+
+        @pl.when(i == 2)
+        def _():
+            wait_x(1, hy)
+            forward(1, hy, hx, 3)
+            forward(1, hy, sib, 4)
+            wait_x(1, hx)
+            forward(1, hx, sib, 5)
+
+        @pl.when(i == 3)
+        def _():
+            wait_x(0, hx + to_sib)
+            wait_x(1, hx + to_sib)
+
+        @pl.when(i == 5)
+        def _():
+            wait_x(0, hd)
+            forward(0, hd, sib, 6)
+            wait_x(1, hd)
+            forward(1, hd, sib, 6)
+            wait_x(0, hy + to_sib)
+            wait_x(1, hy + to_sib)
+
+        @pl.when(i == 7)
+        def _():
+            wait_x(0, hd + to_sib)
+            wait_x(1, hd + to_sib)
+
+        index = chip_at((i // 2) % 2, i // 4) + (i % 2) * to_sib
         for which in range(3):
-            project(which, index, False)
-
-    project(0, h, True)
-    project(1, h, True)
-    wait_x(0, hx)
-    forward(0, hx, hy, 3)
-    forward(0, hx, sib, 4)
-    wait_x(0, hy)
-    forward(0, hy, sib, 5)
-    project(2, h, True)
-    wait_x(1, hy)
-    forward(1, hy, hx, 3)
-    forward(1, hy, sib, 4)
-    wait_x(1, hx)
-    forward(1, hx, sib, 5)
-    wait_x(0, sib)
-    wait_x(1, sib)
-    project_all(sib)
-    project_all(hx)
-    wait_x(0, hd)
-    forward(0, hd, sib, 6)
-    wait_x(1, hd)
-    forward(1, hd, sib, 6)
-    project_all(hy)
-    for index in (hx + to_sib, hy + to_sib):
-        wait_x(0, index)
-        wait_x(1, index)
-        project_all(index)
-    project_all(hd)
-    wait_x(0, hd + to_sib)
-    wait_x(1, hd + to_sib)
-    project_all(hd + to_sib)
+            weight_copy(which, index).wait()
+            left = xbuf[0 if which < 2 else 1, index]
+            for begin, size in strips(units, 2 * LANES):
+                acc[which, :, begin : begin + size] += dot(
+                    left, weights[which, index, begin : begin + size, :], NT
+                )
+
     x_copy = pltpu.make_async_copy(xbuf.at[0], x_out, out_sem.at[0])
     x_copy.start()
 
@@ -446,10 +459,12 @@
         hit = (source_rank >= 0.0) & (slot_value == source_rank + float(CAP * source))
         slot_prob = slot_prob + jnp.sum(jnp.where(hit, source_prob, 0.0), axis=1, keepdims=True)
 
-    router = jnp.zeros((slots, LANES), F32)
     slot_prob = jnp.broadcast_to(slot_prob, (slots, LANES))
-    for begin, size in strips(units, LANES):
-        part = slice(begin, begin + size)
+    router_sum[...] = jnp.zeros_like(router_sum)
+
+    @pl.loop(0, units // LANES)
+    def _(i):
+        part = pl.ds(pl.multiple_of(i * LANES, LANES), LANES)
         gate_pre = acc[0, :, part]
         up_pre = acc[1, :, part]
         back_pre = acc[2, :, part]
@@ -460,10 +475,11 @@
             scaled * up_pre * sigmoid_gate * (1.0 + gate_pre * (1.0 - sigmoid_gate))
         ).astype(BF16)
         dbuf[1, :, part] = (scaled * silu_gate).astype(BF16)
-        router = router + silu_gate * up_pre * back_pre
+        router_sum[...] += silu_gate * up_pre * back_pre
+
     d_copy = pltpu.make_async_copy(dbuf, d_out, out_sem.at[1])
     d_copy.start()
-    router = jnp.broadcast_to(jnp.sum(router, axis=1, keepdims=True), (slots, LANES))
+    router = jnp.broadcast_to(jnp.sum(router_sum[...], axis=1, keepdims=True), (slots, LANES))
     if slots < LANES:
         router = jnp.concatenate([router, jnp.zeros((LANES - slots, LANES), F32)], axis=0)
     q_send[0] = router.T[0:8, :]
@@ -477,50 +493,67 @@
             dbuf[1], weights[1, index, :, part], NN
         )
 
-    chips = (hd, hx, hy, h)
-
-    def sibling_part(slot):
-        for begin, size in column_strips:
-            one_send[slot, :, begin : begin + size] = partial(
-                chips[slot] + to_sib, begin, size
-            ).astype(BF16)
-        send(
-            one_send.at[slot],
-            one_recv.at[slot],
-            one_send_sem.at[slot],
-            one_recv_sem.at[slot],
-            at_hidden(sib),
-        )
-
-    sibling_part(0)
-    arrived(q_recv.at[0], q_send_sem.at[0], q_recv_sem.at[0])
-    q_send[1] = q_send[0] + q_recv[0]
-    for slot, index in enumerate((hd, hx, hy)):
-        send(
-            q_send.at[1],
-            q_recv.at[1 + slot],
-            q_send_sem.at[1 + slot],
-            q_recv_sem.at[1 + slot],
-            at_hidden(index),
-        )
-    for slot, index in enumerate(chips):
-        if slot < 3:
-            sibling_part(slot + 1)
-        for begin, size in column_strips:
-            own_part[:, begin : begin + size] = partial(index, begin, size)
-        arrived(one_recv.at[slot], one_send_sem.at[slot], one_recv_sem.at[slot])
-        total = own_part[...] + one_recv[slot].astype(F32)
-        if slot == 3:
-            own_part[...] = total
-        else:
-            two_send[slot] = total.astype(BF16)
-            send(
-                two_send.at[slot],
-                two_recv.at[slot],
-                two_send_sem.at[slot],
-                two_recv_sem.at[slot],
-                at_hidden(index),
+    def chip_of(slot):
+        return chip_at((3 - slot) // 2, (3 - slot) % 2)
+
+    @pl.loop(0, 5)
+    def _(turn):
+        @pl.when(turn < 4)
+        def _():
+            for begin, size in column_strips:
+                one_send[turn, :, begin : begin + size] = partial(
+                    chip_of(turn) + to_sib, begin, size
+                ).astype(BF16)
+            start(
+                one_send.at[turn],
+                one_recv.at[turn],
+                one_send_sem.at[turn],
+                one_recv_sem.at[turn],
+                at_hidden(sib),
             )
+
+        @pl.when(turn == 1)
+        def _():
+            arrived(q_recv.at[0], q_send_sem.at[0], q_recv_sem.at[0])
+            q_send[1] = q_send[0] + q_recv[0]
+            for place, index in enumerate((hd, hx, hy)):
+                start(
+                    q_send.at[1],
+                    q_recv.at[1 + place],
+                    q_send_sem.at[1 + place],
+                    q_recv_sem.at[1 + place],
+                    at_hidden(index),
+                )
+
+        @pl.when(turn > 0)
+        def _():
+            slot = turn - 1
+            index = chip_of(slot)
+            for begin, size in column_strips:
+                own_part[:, begin : begin + size] = partial(index, begin, size)
+            arrived(one_recv.at[slot], one_send_sem.at[slot], one_recv_sem.at[slot])
+            own_part[...] += one_recv[slot].astype(F32)
+
+            @pl.when(slot < 3)
+            def _():
+                two_send[slot] = own_part[...].astype(BF16)
+                start(
+                    two_send.at[slot],
+                    two_recv.at[slot],
+                    two_send_sem.at[slot],
+                    two_recv_sem.at[slot],
+                    at_hidden(index),
+                )
+
+    for a in range(2):
+        for slot in range(3, 7):
+            pending.append((xbuf.at[a, h], x_send.at[a, slot]))
+    for slot in range(3):
+        pending.append((q_send.at[1], q_send_sem.at[1 + slot]))
+    for slot in range(4):
+        pending.append((one_send.at[slot], one_send_sem.at[slot]))
+    for slot in range(3):
+        pending.append((two_send.at[slot], two_send_sem.at[slot]))
 
     for slot in range(3):
         arrived(q_recv.at[1 + slot], q_send_sem.at[1 + slot], q_recv_sem.at[1 + slot])
@@ -584,8 +617,15 @@
             BF16
         )
 
-    for copy in pending:
-        copy.wait_send()
+    for source, send_sem in pending:
+        pltpu.make_async_remote_copy(
+            src_ref=source,
+            dst_ref=source,
+            send_sem=send_sem,
+            recv_sem=send_sem,
+            device_id=at_hidden(sib),
+            device_id_type=MESH,
+        ).wait_send()
     x_copy.wait()
     d_copy.wait()
 
@@ -644,6 +684,7 @@
             dma((dp_count,)),
             dma((dp_count,)),
             pltpu.VMEM((3, slots, units), F32),
+            pltpu.VMEM((slots, LANES), F32),
             pltpu.VMEM((2, slots, units), BF16),
             pltpu.VMEM((4, slots, width), BF16),
             pltpu.VMEM((4, slots, width), BF16),

time: 48.2 us -> 48.6 us (level)
  no operation moved by 1% of the time
where the time goes in v4:
time: 48.6 us; the launch traced here: 48.2 us
  Pallas kernels  47.6 us (98%)
  between operations  0.64 us (1%)
    pallas_call x1, Pallas kernels, fused_body(): pl.pallas_call(functools.partial(fused_kernel, dp_count, owners), out_sha...  38.3 us
    pallas_call x1, Pallas kernels, fused_body(): pl.pallas_call(outer_kernel, grid=(units // LANES,), out_shape=(jax.Shape...  9.32 us

profile of v4, /device:TPU:0, one launch (start us, length us, event | category | flops | bytes accessed | tf_op | source)
XLA Modules:
  0.0 48.2 jit_solution(2108679227233675929)
XLA Ops:
  0.6 38.3 %shard_map.102 = (bf16[32,512]{1,0:T(8,128)(2,1)}, f32[2,32]{1,0:T(2,128)}, bf16[8,80,512]{2,1,0:T(8,128)(2,1)}, bf16[2,80,896]{2,1,0:T(8,128)(2,1)}) custom-call(s32[2,32]{1,0:T(2,128)} %bitcast.3, bf16[2,32]{1,0:T(2,128)(2,1)} %bitcast.4, bf16[32,512]{1,0:T(8,128)(2,1)} %tokens_hbm.1, bf16[32,512]{1,0:T(8,128)(2,1)} %grads_hbm.1, ...), custom_call_target="tpu_custom_call" | custom-call | tf_op jit(solution)/shard_map/pallas_call | solution.py:662
  38.9 9.3 %shard_map.103 = (bf16[896,4096]{1,0:T(8,128)(2,1)}, bf16[896,4096]{1,0:T(8,128)(2,1)}, bf16[32,512]{1,0:T(8,128)(2,1)}, f32[2,32]{1,0:T(2,128)}) custom-call(bf16[2,80,896]{2,1,0:T(8,128)(2,1)} %get-tuple-element.12.d_ref, bf16[8,80,512]{2,1,0:T(8,128)(2,1)} %get-tuple-element.13.x_ref, bf16[32,512]{1,0:T(8,128)(2,1)} %get-tuple-element.14.tokens_ref, ...), custom_call_target="tpu_custom_call" | custom-call | tf_op jit(solution)/shard_map/pallas_call | solution.py:721

commit v5 on v4

--- a/solution.py
+++ b/solution.py
@@ -142,10 +142,7 @@
 def fused_kernel(
     dp_count,
     owners,
-    routes_hbm,
-    probs_hbm,
-    tokens_hbm,
-    grads_hbm,
+    in_ref,
     gate_hbm,
     up_hbm,
     down_hbm,
@@ -191,13 +188,9 @@
     qz_send_sem,
     qz_recv_sem,
     out_sem,
-    routes_ref,
-    probs_ref,
-    tokens_ref,
-    grads_ref,
-    in_sem,
 ):
-    rows, width = tokens_ref.shape
+    width = in_ref.shape[1]
+    rows = (in_ref.shape[0] - 16) // 2
     units = gate_hbm.shape[0]
     groups = width // LANES
     packed = CAP * groups
@@ -223,20 +216,6 @@
         other = (plane + step) % dp_count
         return other, (other, h)
 
-    inputs = [
-        pltpu.make_async_copy(source, target, in_sem.at[n])
-        for n, (source, target) in enumerate(
-            (
-                (routes_hbm, routes_ref),
-                (probs_hbm, probs_ref),
-                (tokens_hbm, tokens_ref),
-                (grads_hbm, grads_ref),
-            )
-        )
-    ]
-    for copy in inputs:
-        copy.start()
-
     barrier = pltpu.get_barrier_semaphore()
     for index in (sib, hx, hy, hd):
         pl.semaphore_signal(barrier, inc=1, device_id=at_hidden(index), device_id_type=MESH)
@@ -288,11 +267,11 @@
     owner_of = jnp.full((8, rows), -1, jnp.int32)
     for j, owner in enumerate(owners):
         owner_of = jnp.where(block_row == j, owner, owner_of)
-    inputs[0].wait()
-    inputs[1].wait()
-    first = jnp.broadcast_to(routes_ref[0:1, :], (8, rows))
-    second = jnp.broadcast_to(routes_ref[1:2, :], (8, rows))
-    prob_rows = probs_ref[...].astype(F32)
+    small = in_ref[2 * rows : 2 * rows + 16, 0:LANES].astype(F32)[:, 0:rows]
+    route_rows = small[0:2, :].astype(jnp.int32)
+    first = jnp.broadcast_to(route_rows[0:1, :], (8, rows))
+    second = jnp.broadcast_to(route_rows[1:2, :], (8, rows))
+    prob_rows = small[2:4, :]
     match = (owner_of == first) | (owner_of == second)
     earlier = lax.broadcasted_iota(jnp.int32, (rows, rows), 0) < lax.broadcasted_iota(
         jnp.int32, (rows, rows), 1
@@ -325,10 +304,10 @@
         axis=0,
     ).astype(BF16)
 
-    for a, ref in enumerate((tokens_ref, grads_ref)):
-        inputs[2 + a].wait()
+    for a in range(2):
+        values = in_ref[a * rows : (a + 1) * rows, :]
         stacked = jnp.concatenate(
-            [ref[:, n * LANES : (n + 1) * LANES] for n in range(groups)], axis=0
+            [values[:, n * LANES : (n + 1) * LANES] for n in range(groups)], axis=0
         )
         zsend[a] = dot(select, stacked, NN).astype(BF16).reshape(dp_count, packed, LANES)
         zrecv[a, plane] = zsend[a, plane]
@@ -605,7 +584,7 @@
         column = jnp.broadcast_to(q_columns[:, j : j + 1], wanted.shape)
         value = jnp.sum(jnp.where(hit, column, 0.0), axis=0, keepdims=True)
         for k in range(2):
-            found[k] = found[k] + jnp.where(routes_ref[k : k + 1, :] == owner, value, 0.0)
+            found[k] = found[k] + jnp.where(route_rows[k : k + 1, :] == owner, value, 0.0)
     grad_probs_ref[...] = jnp.concatenate(found, axis=0)
 
     for step in range(1, dp_count):
@@ -659,6 +638,18 @@
     dma = pltpu.SemaphoreType.DMA
     vmem = pl.BlockSpec(memory_space=pltpu.VMEM)
     anywhere = pl.BlockSpec(memory_space=pl.ANY)
+    packed_in = sum(
+        jnp.pad(
+            part.astype(BF16),
+            ((first, 2 * rows + 16 - first - part.shape[0]), (0, width - part.shape[1])),
+        )
+        for first, part in (
+            (0, tokens),
+            (rows, grad_out),
+            (2 * rows, routes.T),
+            (2 * rows + 2, probs.T),
+        )
+    )
     grad_tokens, grad_probs, x_all, d_all = pl.pallas_call(
         functools.partial(fused_kernel, dp_count, owners),
         out_shape=(
@@ -667,7 +658,7 @@
             jax.ShapeDtypeStruct((hidden_count, slots, width), BF16),
             jax.ShapeDtypeStruct((2, slots, units), BF16),
         ),
-        in_specs=[pl.BlockSpec(memory_space=pltpu.HBM)] * 7,
+        in_specs=[vmem] + [anywhere] * 3,
         out_specs=(vmem, vmem, anywhere, anywhere),
         scratch_shapes=[
             pltpu.VMEM((3, hidden_count, units, width), BF16),
@@ -708,16 +699,11 @@
             dma((dp_count,)),
             dma((dp_count,)),
             dma((2,)),
-            pltpu.VMEM((2, rows), jnp.int32),
-            pltpu.VMEM((2, rows), BF16),
-            pltpu.VMEM((rows, width), BF16),
-            pltpu.VMEM((rows, width), BF16),
-            dma((4,)),
         ],
         compiler_params=pltpu.CompilerParams(
-            collective_id=0, has_side_effects=True, vmem_limit_bytes=64 << 20
+            collective_id=0, has_side_effects=True, vmem_limit_bytes=48 << 20
         ),
-    )(routes.T, probs.T, tokens, grad_out, gate_weight, up_weight, down_weight)
+    )(packed_in, gate_weight, up_weight, down_weight)
     grad_gate, grad_up, grad_tokens, grad_probs = pl.pallas_call(
         outer_kernel,
         grid=(units // LANES,),
@@ -739,7 +725,7 @@
             pl.BlockSpec((rows, width), lambda i: (0, 0)),
             pl.BlockSpec((2, rows), lambda i: (0, 0)),
         ),
-        compiler_params=pltpu.CompilerParams(vmem_limit_bytes=64 << 20),
+        compiler_params=pltpu.CompilerParams(vmem_limit_bytes=48 << 20),
     )(d_all, x_all, grad_tokens, grad_probs)
     return (grad_tokens, grad_probs.T, grad_gate, grad_up)
 

time: 48.6 us -> 48.5 us (level)
  Pallas kernels: 47.6 us -> 46.1 us
  other arithmetic: 0 us -> 1.48 us
    pallas_call x1, Pallas kernels: 9.32 us -> 8.27 us  [fused_body(): pl.pallas_call(outer_kernel, grid=(units // LANES,), out_shape=(jax.Shape...]
    add x0 -> x1, other arithmetic: none -> 0.8 us  [fused_body(): sum((jnp.pad(part.astype(BF16), ((first, 2 * rows + 16 - first - part.sha...]
    convert_element_type x0 -> x1, other arithmetic: none -> 0.68 us  [fused_body(): part.astype(BF16)]
where the time goes in v5:
time: 48.5 us; the launch traced here: 48.3 us
  Pallas kernels  46.1 us (95%)
  other arithmetic  1.48 us (3%)
  between operations  0.64 us (1%)
    pallas_call x1, Pallas kernels, fused_body(): pl.pallas_call(functools.partial(fused_kernel, dp_count, owners), out_sha...  37.9 us
    pallas_call x1, Pallas kernels, fused_body(): pl.pallas_call(outer_kernel, grid=(units // LANES,), out_shape=(jax.Shape...  8.27 us

profile of v5, /device:TPU:0, one launch (start us, length us, event | category | flops | bytes accessed | tf_op | source)
XLA Modules:
  0.0 48.3 jit_solution(16040096176549047157)
XLA Ops:
  0.6 0.7 %convert_bitcast_fusion = bf16[2,32]{1,0:T(2,128)(2,1)S(1)} fusion(s32[32,2]{0,1:T(2,128)} %param.9), kind=kLoop, calls=%fused_computation.1 | loop fusion | flops 64 | bytes 384 | tf_op jit(solution)/shard_map/convert_element_type | solution.py:643
  1.3 0.8 %pad_add_fusion.in_ref = bf16[80,512]{1,0:T(8,128)(2,1)S(1)} fusion(bf16[2,32]{1,0:T(2,128)(2,1)} %bitcast.4, bf16[2,32]{1,0:T(2,128)(2,1)S(1)} %convert_bitcast_fusion, bf16[32,512]{1,0:T(8,128)(2,1)} %param.8, bf16[32,512]{1,0:T(8,128)(2,1)} %param.7), kind=kLoop, calls=%fused_computation | loop fusion | flops 327680 | bytes 147712 | tf_op jit(solution)/shard_map/add | solution.py:641
  2.1 37.9 %shard_map.102 = (bf16[32,512]{1,0:T(8,128)(2,1)S(1)}, f32[2,32]{1,0:T(2,128)S(1)}, bf16[8,80,512]{2,1,0:T(8,128)(2,1)S(1)}, bf16[2,80,896]{2,1,0:T(8,128)(2,1)S(1)}) custom-call(bf16[80,512]{1,0:T(8,128)(2,1)S(1)} %pad_add_fusion.in_ref, bf16[896,4096]{1,0:T(8,128)(2,1)} %gate_hbm.1, bf16[896,4096]{1,0:T(8,128)(2,1)} %up_hbm.1, bf16[896,4096]{1,0:T(8,128)(2,1)} %down_hbm.1), custom_call_target="tpu_custom_call" | custom-call | tf_op jit(solution)/shard_map/pallas_call | solution.py:653
  40.0 8.3 %shard_map.103 = (bf16[896,4096]{1,0:T(8,128)(2,1)}, bf16[896,4096]{1,0:T(8,128)(2,1)}, bf16[32,512]{1,0:T(8,128)(2,1)}, f32[2,32]{1,0:T(2,128)}) custom-call(bf16[2,80,896]{2,1,0:T(8,128)(2,1)S(1)} %get-tuple-element.12.d_ref, bf16[8,80,512]{2,1,0:T(8,128)(2,1)S(1)} %get-tuple-element.13.x_ref, bf16[32,512]{1,0:T(8,128)(2,1)S(1)} %get-tuple-element.14.tokens_ref, ...), custom_call_target="tpu_custom_call" | custom-call | tf_op jit(solution)/shard_map/pallas_call | solution.py:707
